TPU v7x, 512 devices: a whole 4x4x16 slice. The times are simulated.
512 devices in a mesh: seq: 64 (over z, y_lo, core), tp: 8 (over x, y_hi).
Axes of the slice: x: 4, y: 4 (y_hi: 2, y_lo: 2; y = y_hi * 2 + y_lo), z: 16, core: 2. Of those that a mesh axis runs over, the one named last changes fastest.
Arguments:
- query: bfloat16 [8192, 2048], P('seq', 'tp'), may hold values from -5 to 5
- key: bfloat16 [8192, 2048], P('seq', 'tp'), may hold values from -5 to 5
- value: bfloat16 [8192, 2048], P('seq', 'tp'), may hold values from -6 to 6
- documents: int32 [64], P('seq'), may hold values from 1 to 64, as said below
- frames: int32 [64], P('seq'), may hold values 0 or 1
- out_cotangent: bfloat16 [8192, 4096], P(('seq', 'tp')), may hold values from -6 to 6
- output_weight: bfloat16 [2048, 4096], P('tp'), may hold values from -0.125 to 0.125
Outputs:
- attended: bfloat16 [8192, 2048], P('seq', 'tp')
- query_grads: bfloat16 [8192, 2048], P('seq', 'tp')
- key_grads: bfloat16 [8192, 2048], P('seq', 'tp')
- value_grads: bfloat16 [8192, 2048], P('seq', 'tp')
Inputs may be any that keep to these rules, and one draw needn't show every extreme that they name: documents never falls along the window; a tile's id is one plus the index of its document's first tile; a new document begins at the first tile of each aligned stretch of 2048 tokens and at the last tile of the window.
All inputs are finite; a program needn't handle non-finite values. No bound on the sum of `frames` on one device may be relied on, other than what follows from the above.
Results may differ from a plain program's by a relative error of at most 0.035.
Values may be sent and summed in bfloat16 or wider, within the bound.
A program may use at most 64 MiB of HBM per device.

v0:
```python
import jax
import jax.numpy as jnp
from jax import lax
from jax.sharding import PartitionSpec as P

HEAD_DIM = 128
TILE = 128
SPAN = 16


far_below = -1e30


def shifted(block, axis, distance):
    devices = range(lax.axis_size(axis))
    route = [(i - distance, i) for i in devices if i - distance in devices]
    return lax.ppermute(block, axis, route)


def token_level(tiles):
    return jnp.broadcast_to(tiles[:, None], (tiles.shape[0], TILE)).reshape(-1)


def split_heads(rows_in):
    return rows_in.reshape(rows_in.shape[0], -1, HEAD_DIM)


def join_heads(heads):
    return heads.transpose(1, 0, 2).reshape(heads.shape[1], -1).astype(jnp.bfloat16)


def visible_pairs(query_place, query_document, query_frame, key_place, key_document):
    same_document = query_document[:, None] == key_document[None, :]
    earlier = key_place[None, :] <= query_place[:, None]
    same_tile = query_place[:, None] // TILE == key_place[None, :] // TILE
    return same_document & (earlier | same_tile & (query_frame[:, None] == 1))


def scores_of(query_heads, key_heads, mask):
    raw = jnp.einsum(
        "qhd,khd->hqk", query_heads, key_heads, preferred_element_type=jnp.float32
    ) * HEAD_DIM ** (-0.5)
    return jnp.where(mask[None], raw, far_below)


def absorb(state, query_heads, key_heads, value_heads, mask):
    top, total, summed = state
    scores = scores_of(query_heads, key_heads, mask)
    new_top = jnp.maximum(top, jnp.max(scores, axis=2))
    weights = jnp.where(mask[None], jnp.exp(scores - new_top[:, :, None]), 0.0)
    factor = jnp.exp(top - new_top)
    total = factor * total + jnp.sum(weights, axis=2)
    summed = factor[:, :, None] * summed + jnp.einsum(
        "hqk,khd->hqd",
        weights.astype(jnp.bfloat16),
        value_heads,
        preferred_element_type=jnp.float32,
    )
    return (new_top, total, summed)


def chances_of(query_heads, key_heads, mask, log_total):
    scores = scores_of(query_heads, key_heads, mask)
    return jnp.where(mask[None], jnp.exp(scores - log_total[:, :, None]), 0.0)


def slopes_of(chances, grad_heads, value_heads, delta):
    pushes = jnp.einsum("qhd,khd->hqk", grad_heads, value_heads, preferred_element_type=jnp.float32)
    return (HEAD_DIM ** (-0.5) * chances * (pushes - delta[:, :, None])).astype(jnp.bfloat16)


def on_device(query, key, value, documents, frames, out_cotangent, output_weight):
    rows = query.shape[0]
    base = lax.axis_index("seq") * rows
    own_place = base + jnp.arange(rows, dtype=jnp.int32)
    own_document = token_level(documents)
    own_frame = token_level(frames)
    query_heads = split_heads(query)
    key_heads = split_heads(key)
    value_heads = split_heads(value)
    heads_here = query_heads.shape[1]
    grad_rows = lax.dot_general(
        lax.all_gather(out_cotangent, "tp", axis=0, tiled=True),
        output_weight,
        (((1,), (1,)), ((), ())),
        preferred_element_type=jnp.float32,
    ).astype(jnp.bfloat16)
    grad_heads = split_heads(grad_rows)

    def key_mask(key_document, key_start):
        key_place = key_start + jnp.arange(key_document.shape[0], dtype=jnp.int32)
        return visible_pairs(own_place, own_document, own_frame, key_place, key_document)

    def forward_piece(state, key_rows, value_rows, key_document, key_start):
        mask = key_mask(key_document, key_start)
        return absorb(state, query_heads, split_heads(key_rows), split_heads(value_rows), mask)

    def pass_keys(blocks):
        return shifted((blocks[0], blocks[1], blocks[2]), "seq", 1)

    empty = jnp.zeros((heads_here, rows), jnp.float32)
    zero_heads = jnp.zeros((heads_here, rows, HEAD_DIM), jnp.float32)
    start_state = (jnp.full((heads_here, rows), far_below, jnp.float32), empty, zero_heads)
    kept = ()
    state = forward_piece(start_state, key, value, own_document, base)

    def forward_step(number, carry):
        current, blocks, stored = carry
        blocks = pass_keys(blocks)
        current = forward_piece(
            current, blocks[0], blocks[1], blocks[2], base - (number + 1) * rows
        )
        return (current, blocks, stored)

    state, last_blocks, kept = lax.fori_loop(
        0, SPAN - 1, forward_step, (state, (key, value, own_document), kept)
    )
    top, total, summed = state
    log_total = top + jnp.log(total)
    attended = join_heads(summed / total[:, :, None])
    delta = jnp.einsum(
        "qhd,qhd->hq", grad_heads, split_heads(attended), preferred_element_type=jnp.float32
    )

    def query_piece(grad_sum, key_rows, value_rows, key_document, key_start):
        mask = key_mask(key_document, key_start)
        nearby = split_heads(key_rows)
        chances = chances_of(query_heads, nearby, mask, log_total)
        slopes = slopes_of(chances, grad_heads, split_heads(value_rows), delta)
        return grad_sum + jnp.einsum(
            "hqk,khd->hqd", slopes, nearby, preferred_element_type=jnp.float32
        )

    def key_piece(
        grads, query_rows, grad_visit, query_document, query_total, query_delta, query_start
    ):
        query_place = query_start + jnp.arange(rows, dtype=jnp.int32)
        mask = visible_pairs(query_place, query_document, own_frame, own_place, own_document)
        visit_heads = split_heads(query_rows)
        visit_grads = split_heads(grad_visit)
        chances = chances_of(visit_heads, key_heads, mask, query_total)
        slopes = slopes_of(chances, visit_grads, value_heads, query_delta)
        key_sum = grads[0] + jnp.einsum(
            "hqk,qhd->hkd", slopes, visit_heads, preferred_element_type=jnp.float32
        )
        value_sum = grads[1] + jnp.einsum(
            "hqk,qhd->hkd",
            chances.astype(jnp.bfloat16),
            visit_grads,
            preferred_element_type=jnp.float32,
        )
        return (key_sum, value_sum)

    local_mask = key_mask(own_document, base)
    chances = chances_of(query_heads, key_heads, local_mask, log_total)
    slopes = slopes_of(chances, grad_heads, value_heads, delta)
    query_sum = jnp.einsum("hqk,khd->hqd", slopes, key_heads, preferred_element_type=jnp.float32)
    key_sum = jnp.einsum("hqk,qhd->hkd", slopes, query_heads, preferred_element_type=jnp.float32)
    value_sum = jnp.einsum(
        "hqk,qhd->hkd", chances.astype(jnp.bfloat16), grad_heads, preferred_element_type=jnp.float32
    )

    def again_step(number, carry):
        current, blocks = carry
        blocks = pass_keys(blocks)
        return (
            query_piece(current, blocks[0], blocks[1], blocks[2], base - (number + 1) * rows),
            blocks,
        )

    query_sum, last_again = lax.fori_loop(
        0, SPAN - 1, again_step, (query_sum, (key, value, own_document))
    )

    def query_step(number, carry):
        grads, blocks, moments = carry
        blocks = shifted((blocks[0], blocks[1]), "seq", -1)
        moments = shifted((moments[0], moments[1], moments[2]), "seq", -1)
        grads = key_piece(
            grads,
            blocks[0],
            blocks[1],
            moments[2],
            moments[0],
            moments[1],
            base + (number + 1) * rows,
        )
        return (grads, blocks, moments)

    grads, last_queries, last_moments = lax.fori_loop(
        0,
        SPAN - 1,
        query_step,
        ((key_sum, value_sum), (query, grad_rows), (log_total, delta, own_document)),
    )
    return (attended, join_heads(query_sum), join_heads(grads[0]), join_heads(grads[1]))


def solution(mesh):
    in_specs = (
        P("seq", "tp"),
        P("seq", "tp"),
        P("seq", "tp"),
        P("seq"),
        P("seq"),
        P(("seq", "tp"), None),
        P("tp", None),
    )
    out_specs = (P("seq", "tp"), P("seq", "tp"), P("seq", "tp"), P("seq", "tp"))
    return jax.shard_map(
        on_device, mesh=mesh, in_specs=in_specs, out_specs=out_specs, check_vma=False
    )
```

profile of v0, /device:TPU:473, one launch (start us, length us, event | category | flops | bytes accessed | tf_op | source)
XLA Modules:
  0.0 639.9 jit_solution(16410668605132422909)
XLA Ops:
  15.0 159.2 %while.82 = (s32[]{:T(128)}, f32[2,128]{1,0:T(2,128)S(1)}, f32[2,128]{1,0:T(2,128)S(1)}, f32[2,128,128]{2,1,0:T(8,128)S(1)}, bf16[128,256]{0,1:T(8,128)(2,1)S(1)...) while((s32[]{:T(128)}, f32[2,128]{1,0:T(2,128)S(1)}, ...), condition=%wide.region_5.6_spmd.clone.clone, body=%wide.region_2.5_spmd.clone.clone.sunk | while | flops 17224452 | bytes 1728547 | solution.py:115
  25.2 5.2 collective-permute-start
  35.9 5.2 collective-permute-start
  46.5 5.2 collective-permute-start
  57.1 5.3 collective-permute-start
  67.9 5.1 collective-permute-start
  78.5 5.2 collective-permute-start
  89.1 5.2 collective-permute-start
  99.8 5.2 collective-permute-start
  110.4 5.2 collective-permute-start
  121.0 5.2 collective-permute-start
  131.7 5.2 collective-permute-start
  142.3 5.2 collective-permute-start
  152.9 5.2 collective-permute-start
  163.6 5.2 collective-permute-start
  178.1 156.6 %while.83 = (s32[]{:T(128)}, f32[2,128,128]{2,1,0:T(8,128)S(1)}, bf16[128,256]{0,1:T(8,128)(2,1)S(1)}, bf16[128,256]{1,0:T(8,128)(2,1)S(1)}, s32[128]{0:T(128)S(...) while((s32[]{:T(128)}, f32[2,128,128]{2,1,0:T(8,128)S(1)}, ...), condition=%wide.region_7.8_spmd.clone.clone, body=%wide.region_6.7_spmd.clone.clone.sunk | while | flops 25547012 | bytes 1746987 | solution.py:171
  178.1 5.2 collective-permute-start.3
  189.0 4.7 collective-permute-start.3
  199.4 4.7 collective-permute-start.3
  209.8 4.7 collective-permute-start.3
  220.2 4.7 collective-permute-start.3
  230.6 4.7 collective-permute-start.3
  241.0 4.7 collective-permute-start.3
  251.5 4.7 collective-permute-start.3
  261.9 4.7 collective-permute-start.3
  272.3 4.7 collective-permute-start.3
  282.7 4.7 collective-permute-start.3
  293.1 4.7 collective-permute-start.3
  303.5 4.7 collective-permute-start.3
  313.9 4.7 collective-permute-start.3
  324.3 4.7 collective-permute-start.3
  335.4 296.4 %while.84 = (s32[]{:T(128)}, f32[2,128,128]{2,1,0:T(8,128)S(1)}, f32[2,128,128]{2,1,0:T(8,128)S(1)}, bf16[128,256]{0,1:T(8,128)(2,1)S(1)}, bf16[128,256]{0,1:T(8...) while((s32[]{:T(128)}, f32[2,128,128]{2,1,0:T(8,128)S(1)}, ...), condition=%wide.region_9.10_spmd.clone.clone, body=%wide.region_8.9_spmd.clone.clone.sunk | while | flops 34001156 | bytes 2152579 | solution.py:190
  335.4 5.0 collective-permute-start.6
  340.3 5.8 collective-permute-start.7
  346.1 6.4 collective-permute-start.8
  352.5 5.8 collective-permute-start.9
  358.2 6.4 collective-permute-start.10
  367.1 5.8 collective-permute-start.6
  372.8 6.4 collective-permute-start.7
  379.2 5.8 collective-permute-start.8
  385.0 6.4 collective-permute-start.9
  391.3 5.8 collective-permute-start.10
  399.6 6.4 collective-permute-start.6
  412.1 4.2 collective-permute-start.9
  431.0 4.2 collective-permute-start.9
  478.7 4.2 collective-permute-start.8
  553.5 4.2 collective-permute-start.9
  572.3 4.2 collective-permute-start.9
  (850 shorter events, 359.4 us)
Async XLA Ops:
  7.2 167.1 %all-gather.2.cloned.1.call-start = ((), (), s32[]{:S(2)}) async-start(), calls=%async_computation | async-start | bytes 1179648 | tf_op jit(solution)/shard_map/all_gather | solution.py:83
  178.1 10.5 %collective-permute-start.3 = (bf16[128,256]{0,1:T(8,128)(2,1)S(1)}, bf16[128,256]{0,1:T(8,128)(2,1)S(1)}, u32[]{:S(2)}, u32[]{:S(2)}) collective-permute-start(bf16[128,256]{0,1:T(8,128)(2,1)S(1)} %get-tuple-element.1755), channel_id=1, source_target_pairs={{0,8},{8,16},{16,24},{24,32},{32,40},{40,48},{48,56},{56,64},{64,7... | collective-permute-start | bytes 196616 | tf_op jit(solution)/shard_map/while/body/eval_jaxpr/ppermute | solution.py:17
  189.0 10.0 %collective-permute-start.3 = (bf16[128,256]{0,1:T(8,128)(2,1)S(1)}, bf16[128,256]{0,1:T(8,128)(2,1)S(1)}, u32[]{:S(2)}, u32[]{:S(2)}) collective-permute-start(bf16[128,256]{0,1:T(8,128)(2,1)S(1)} %get-tuple-element.1755), channel_id=1, source_target_pairs={{0,8},{8,16},{16,24},{24,32},{32,40},{40,48},{48,56},{56,64},{64,7... | collective-permute-start | bytes 196616 | tf_op jit(solution)/shard_map/while/body/eval_jaxpr/ppermute | solution.py:17
  335.4 30.8 %collective-permute-start.6 = (bf16[128,256]{0,1:T(8,128)(2,1)S(1)}, bf16[128,256]{0,1:T(8,128)(2,1)S(1)}, u32[]{:S(2)}, u32[]{:S(2)}) collective-permute-start(bf16[128,256]{0,1:T(8,128)(2,1)S(1)} %get-tuple-element.1799), channel_id=1, source_target_pairs={{8,0},{16,8},{24,16},{32,24},{40,32},{48,40},{56,48},{64,56},{72,6... | collective-permute-start | bytes 196616 | tf_op jit(solution)/shard_map/while/body/eval_jaxpr/ppermute | solution.py:17
  340.3 25.8 %collective-permute-start.7 = (f32[2,128]{1,0:T(2,128)S(1)}, f32[2,128]{1,0:T(2,128)S(1)}, u32[]{:S(2)}, u32[]{:S(2)}) collective-permute-start(f32[2,128]{1,0:T(2,128)S(1)} %get-tuple-element.1801), channel_id=1, source_target_pairs={{8,0},{16,8},{24,16},{32,24},{40,32},{48,40},{56,48},{64,56},{72,6... | collective-permute-start | bytes 3080 | tf_op jit(solution)/shard_map/while/body/eval_jaxpr/ppermute | solution.py:17
  346.1 19.2 %collective-permute-start.8 = (s32[128]{0:T(128)S(1)}, s32[128]{0:T(128)S(1)}, u32[]{:S(2)}, u32[]{:S(2)}) collective-permute-start(s32[128]{0:T(128)S(1)} %get-tuple-element.1803), channel_id=1, source_target_pairs={{8,0},{16,8},{24,16},{32,24},{40,32},{48,40},{56,48},{64,56},{72,6... | collective-permute-start | bytes 1544 | tf_op jit(solution)/shard_map/while/body/eval_jaxpr/ppermute | solution.py:17
  352.5 13.9 %collective-permute-start.9 = (bf16[128,256]{0,1:T(8,128)(2,1)S(1)}, bf16[128,256]{0,1:T(8,128)(2,1)S(1)}, u32[]{:S(2)}, u32[]{:S(2)}) collective-permute-start(bf16[128,256]{0,1:T(8,128)(2,1)S(1)} %get-tuple-element.1800), channel_id=1, source_target_pairs={{8,0},{16,8},{24,16},{32,24},{40,32},{48,40},{56,48},{64,56},{72,6... | collective-permute-start | bytes 196616 | tf_op jit(solution)/shard_map/while/body/eval_jaxpr/ppermute | solution.py:17
  367.1 31.6 %collective-permute-start.6 = (bf16[128,256]{0,1:T(8,128)(2,1)S(1)}, bf16[128,256]{0,1:T(8,128)(2,1)S(1)}, u32[]{:S(2)}, u32[]{:S(2)}) collective-permute-start(bf16[128,256]{0,1:T(8,128)(2,1)S(1)} %get-tuple-element.1799), channel_id=1, source_target_pairs={{8,0},{16,8},{24,16},{32,24},{40,32},{48,40},{56,48},{64,56},{72,6... | collective-permute-start | bytes 196616 | tf_op jit(solution)/shard_map/while/body/eval_jaxpr/ppermute | solution.py:17
  372.8 25.8 %collective-permute-start.7 = (f32[2,128]{1,0:T(2,128)S(1)}, f32[2,128]{1,0:T(2,128)S(1)}, u32[]{:S(2)}, u32[]{:S(2)}) collective-permute-start(f32[2,128]{1,0:T(2,128)S(1)} %get-tuple-element.1801), channel_id=1, source_target_pairs={{8,0},{16,8},{24,16},{32,24},{40,32},{48,40},{56,48},{64,56},{72,6... | collective-permute-start | bytes 3080 | tf_op jit(solution)/shard_map/while/body/eval_jaxpr/ppermute | solution.py:17
  379.2 18.6 %collective-permute-start.8 = (s32[128]{0:T(128)S(1)}, s32[128]{0:T(128)S(1)}, u32[]{:S(2)}, u32[]{:S(2)}) collective-permute-start(s32[128]{0:T(128)S(1)} %get-tuple-element.1803), channel_id=1, source_target_pairs={{8,0},{16,8},{24,16},{32,24},{40,32},{48,40},{56,48},{64,56},{72,6... | collective-permute-start | bytes 1544 | tf_op jit(solution)/shard_map/while/body/eval_jaxpr/ppermute | solution.py:17
  385.0 13.9 %collective-permute-start.9 = (bf16[128,256]{0,1:T(8,128)(2,1)S(1)}, bf16[128,256]{0,1:T(8,128)(2,1)S(1)}, u32[]{:S(2)}, u32[]{:S(2)}) collective-permute-start(bf16[128,256]{0,1:T(8,128)(2,1)S(1)} %get-tuple-element.1800), channel_id=1, source_target_pairs={{8,0},{16,8},{24,16},{32,24},{40,32},{48,40},{56,48},{64,56},{72,6... | collective-permute-start | bytes 196616 | tf_op jit(solution)/shard_map/while/body/eval_jaxpr/ppermute | solution.py:17
  399.6 22.6 %collective-permute-start.6 = (bf16[128,256]{0,1:T(8,128)(2,1)S(1)}, bf16[128,256]{0,1:T(8,128)(2,1)S(1)}, u32[]{:S(2)}, u32[]{:S(2)}) collective-permute-start(bf16[128,256]{0,1:T(8,128)(2,1)S(1)} %get-tuple-element.1799), channel_id=1, source_target_pairs={{8,0},{16,8},{24,16},{32,24},{40,32},{48,40},{56,48},{64,56},{72,6... | collective-permute-start | bytes 196616 | tf_op jit(solution)/shard_map/while/body/eval_jaxpr/ppermute | solution.py:17
  405.9 13.8 %collective-permute-start.7 = (f32[2,128]{1,0:T(2,128)S(1)}, f32[2,128]{1,0:T(2,128)S(1)}, u32[]{:S(2)}, u32[]{:S(2)}) collective-permute-start(f32[2,128]{1,0:T(2,128)S(1)} %get-tuple-element.1801), channel_id=1, source_target_pairs={{8,0},{16,8},{24,16},{32,24},{40,32},{48,40},{56,48},{64,56},{72,6... | collective-permute-start | bytes 3080 | tf_op jit(solution)/shard_map/while/body/eval_jaxpr/ppermute | solution.py:17
  412.1 10.3 %collective-permute-start.9 = (bf16[128,256]{0,1:T(8,128)(2,1)S(1)}, bf16[128,256]{0,1:T(8,128)(2,1)S(1)}, u32[]{:S(2)}, u32[]{:S(2)}) collective-permute-start(bf16[128,256]{0,1:T(8,128)(2,1)S(1)} %get-tuple-element.1800), channel_id=1, source_target_pairs={{8,0},{16,8},{24,16},{32,24},{40,32},{48,40},{56,48},{64,56},{72,6... | collective-permute-start | bytes 196616 | tf_op jit(solution)/shard_map/while/body/eval_jaxpr/ppermute | solution.py:17
  423.1 17.9 %collective-permute-start.6 = (bf16[128,256]{0,1:T(8,128)(2,1)S(1)}, bf16[128,256]{0,1:T(8,128)(2,1)S(1)}, u32[]{:S(2)}, u32[]{:S(2)}) collective-permute-start(bf16[128,256]{0,1:T(8,128)(2,1)S(1)} %get-tuple-element.1799), channel_id=1, source_target_pairs={{8,0},{16,8},{24,16},{32,24},{40,32},{48,40},{56,48},{64,56},{72,6... | collective-permute-start | bytes 196616 | tf_op jit(solution)/shard_map/while/body/eval_jaxpr/ppermute | solution.py:17
  425.0 13.6 %collective-permute-start.7 = (f32[2,128]{1,0:T(2,128)S(1)}, f32[2,128]{1,0:T(2,128)S(1)}, u32[]{:S(2)}, u32[]{:S(2)}) collective-permute-start(f32[2,128]{1,0:T(2,128)S(1)} %get-tuple-element.1801), channel_id=1, source_target_pairs={{8,0},{16,8},{24,16},{32,24},{40,32},{48,40},{56,48},{64,56},{72,6... | collective-permute-start | bytes 3080 | tf_op jit(solution)/shard_map/while/body/eval_jaxpr/ppermute | solution.py:17
  426.9 10.9 %collective-permute-start.8 = (s32[128]{0:T(128)S(1)}, s32[128]{0:T(128)S(1)}, u32[]{:S(2)}, u32[]{:S(2)}) collective-permute-start(s32[128]{0:T(128)S(1)} %get-tuple-element.1803), channel_id=1, source_target_pairs={{8,0},{16,8},{24,16},{32,24},{40,32},{48,40},{56,48},{64,56},{72,6... | collective-permute-start | bytes 1544 | tf_op jit(solution)/shard_map/while/body/eval_jaxpr/ppermute | solution.py:17
  431.0 10.3 %collective-permute-start.9 = (bf16[128,256]{0,1:T(8,128)(2,1)S(1)}, bf16[128,256]{0,1:T(8,128)(2,1)S(1)}, u32[]{:S(2)}, u32[]{:S(2)}) collective-permute-start(bf16[128,256]{0,1:T(8,128)(2,1)S(1)} %get-tuple-element.1800), channel_id=1, source_target_pairs={{8,0},{16,8},{24,16},{32,24},{40,32},{48,40},{56,48},{64,56},{72,6... | collective-permute-start | bytes 196616 | tf_op jit(solution)/shard_map/while/body/eval_jaxpr/ppermute | solution.py:17
  441.9 15.5 %collective-permute-start.6 = (bf16[128,256]{0,1:T(8,128)(2,1)S(1)}, bf16[128,256]{0,1:T(8,128)(2,1)S(1)}, u32[]{:S(2)}, u32[]{:S(2)}) collective-permute-start(bf16[128,256]{0,1:T(8,128)(2,1)S(1)} %get-tuple-element.1799), channel_id=1, source_target_pairs={{8,0},{16,8},{24,16},{32,24},{40,32},{48,40},{56,48},{64,56},{72,6... | collective-permute-start | bytes 196616 | tf_op jit(solution)/shard_map/while/body/eval_jaxpr/ppermute | solution.py:17
  443.9 11.2 %collective-permute-start.7 = (f32[2,128]{1,0:T(2,128)S(1)}, f32[2,128]{1,0:T(2,128)S(1)}, u32[]{:S(2)}, u32[]{:S(2)}) collective-permute-start(f32[2,128]{1,0:T(2,128)S(1)} %get-tuple-element.1801), channel_id=1, source_target_pairs={{8,0},{16,8},{24,16},{32,24},{40,32},{48,40},{56,48},{64,56},{72,6... | collective-permute-start | bytes 3080 | tf_op jit(solution)/shard_map/while/body/eval_jaxpr/ppermute | solution.py:17
  458.4 15.5 %collective-permute-start.6 = (bf16[128,256]{0,1:T(8,128)(2,1)S(1)}, bf16[128,256]{0,1:T(8,128)(2,1)S(1)}, u32[]{:S(2)}, u32[]{:S(2)}) collective-permute-start(bf16[128,256]{0,1:T(8,128)(2,1)S(1)} %get-tuple-element.1799), channel_id=1, source_target_pairs={{8,0},{16,8},{24,16},{32,24},{40,32},{48,40},{56,48},{64,56},{72,6... | collective-permute-start | bytes 196616 | tf_op jit(solution)/shard_map/while/body/eval_jaxpr/ppermute | solution.py:17
  460.3 11.2 %collective-permute-start.7 = (f32[2,128]{1,0:T(2,128)S(1)}, f32[2,128]{1,0:T(2,128)S(1)}, u32[]{:S(2)}, u32[]{:S(2)}) collective-permute-start(f32[2,128]{1,0:T(2,128)S(1)} %get-tuple-element.1801), channel_id=1, source_target_pairs={{8,0},{16,8},{24,16},{32,24},{40,32},{48,40},{56,48},{64,56},{72,6... | collective-permute-start | bytes 3080 | tf_op jit(solution)/shard_map/while/body/eval_jaxpr/ppermute | solution.py:17
  474.8 18.1 %collective-permute-start.6 = (bf16[128,256]{0,1:T(8,128)(2,1)S(1)}, bf16[128,256]{0,1:T(8,128)(2,1)S(1)}, u32[]{:S(2)}, u32[]{:S(2)}) collective-permute-start(bf16[128,256]{0,1:T(8,128)(2,1)S(1)} %get-tuple-element.1799), channel_id=1, source_target_pairs={{8,0},{16,8},{24,16},{32,24},{40,32},{48,40},{56,48},{64,56},{72,6... | collective-permute-start | bytes 196616 | tf_op jit(solution)/shard_map/while/body/eval_jaxpr/ppermute | solution.py:17
  476.7 13.8 %collective-permute-start.7 = (f32[2,128]{1,0:T(2,128)S(1)}, f32[2,128]{1,0:T(2,128)S(1)}, u32[]{:S(2)}, u32[]{:S(2)}) collective-permute-start(f32[2,128]{1,0:T(2,128)S(1)} %get-tuple-element.1801), channel_id=1, source_target_pairs={{8,0},{16,8},{24,16},{32,24},{40,32},{48,40},{56,48},{64,56},{72,6... | collective-permute-start | bytes 3080 | tf_op jit(solution)/shard_map/while/body/eval_jaxpr/ppermute | solution.py:17
  478.7 11.1 %collective-permute-start.8 = (s32[128]{0:T(128)S(1)}, s32[128]{0:T(128)S(1)}, u32[]{:S(2)}, u32[]{:S(2)}) collective-permute-start(s32[128]{0:T(128)S(1)} %get-tuple-element.1803), channel_id=1, source_target_pairs={{8,0},{16,8},{24,16},{32,24},{40,32},{48,40},{56,48},{64,56},{72,6... | collective-permute-start | bytes 1544 | tf_op jit(solution)/shard_map/while/body/eval_jaxpr/ppermute | solution.py:17
  482.9 10.3 %collective-permute-start.9 = (bf16[128,256]{0,1:T(8,128)(2,1)S(1)}, bf16[128,256]{0,1:T(8,128)(2,1)S(1)}, u32[]{:S(2)}, u32[]{:S(2)}) collective-permute-start(bf16[128,256]{0,1:T(8,128)(2,1)S(1)} %get-tuple-element.1800), channel_id=1, source_target_pairs={{8,0},{16,8},{24,16},{32,24},{40,32},{48,40},{56,48},{64,56},{72,6... | collective-permute-start | bytes 196616 | tf_op jit(solution)/shard_map/while/body/eval_jaxpr/ppermute | solution.py:17
  493.9 17.9 %collective-permute-start.6 = (bf16[128,256]{0,1:T(8,128)(2,1)S(1)}, bf16[128,256]{0,1:T(8,128)(2,1)S(1)}, u32[]{:S(2)}, u32[]{:S(2)}) collective-permute-start(bf16[128,256]{0,1:T(8,128)(2,1)S(1)} %get-tuple-element.1799), channel_id=1, source_target_pairs={{8,0},{16,8},{24,16},{32,24},{40,32},{48,40},{56,48},{64,56},{72,6... | collective-permute-start | bytes 196616 | tf_op jit(solution)/shard_map/while/body/eval_jaxpr/ppermute | solution.py:17
  495.8 13.6 %collective-permute-start.7 = (f32[2,128]{1,0:T(2,128)S(1)}, f32[2,128]{1,0:T(2,128)S(1)}, u32[]{:S(2)}, u32[]{:S(2)}) collective-permute-start(f32[2,128]{1,0:T(2,128)S(1)} %get-tuple-element.1801), channel_id=1, source_target_pairs={{8,0},{16,8},{24,16},{32,24},{40,32},{48,40},{56,48},{64,56},{72,6... | collective-permute-start | bytes 3080 | tf_op jit(solution)/shard_map/while/body/eval_jaxpr/ppermute | solution.py:17
  497.7 10.9 %collective-permute-start.8 = (s32[128]{0:T(128)S(1)}, s32[128]{0:T(128)S(1)}, u32[]{:S(2)}, u32[]{:S(2)}) collective-permute-start(s32[128]{0:T(128)S(1)} %get-tuple-element.1803), channel_id=1, source_target_pairs={{8,0},{16,8},{24,16},{32,24},{40,32},{48,40},{56,48},{64,56},{72,6... | collective-permute-start | bytes 1544 | tf_op jit(solution)/shard_map/while/body/eval_jaxpr/ppermute | solution.py:17
  501.8 10.3 %collective-permute-start.9 = (bf16[128,256]{0,1:T(8,128)(2,1)S(1)}, bf16[128,256]{0,1:T(8,128)(2,1)S(1)}, u32[]{:S(2)}, u32[]{:S(2)}) collective-permute-start(bf16[128,256]{0,1:T(8,128)(2,1)S(1)} %get-tuple-element.1800), channel_id=1, source_target_pairs={{8,0},{16,8},{24,16},{32,24},{40,32},{48,40},{56,48},{64,56},{72,6... | collective-permute-start | bytes 196616 | tf_op jit(solution)/shard_map/while/body/eval_jaxpr/ppermute | solution.py:17
  512.7 15.5 %collective-permute-start.6 = (bf16[128,256]{0,1:T(8,128)(2,1)S(1)}, bf16[128,256]{0,1:T(8,128)(2,1)S(1)}, u32[]{:S(2)}, u32[]{:S(2)}) collective-permute-start(bf16[128,256]{0,1:T(8,128)(2,1)S(1)} %get-tuple-element.1799), channel_id=1, source_target_pairs={{8,0},{16,8},{24,16},{32,24},{40,32},{48,40},{56,48},{64,56},{72,6... | collective-permute-start | bytes 196616 | tf_op jit(solution)/shard_map/while/body/eval_jaxpr/ppermute | solution.py:17
  514.7 11.2 %collective-permute-start.7 = (f32[2,128]{1,0:T(2,128)S(1)}, f32[2,128]{1,0:T(2,128)S(1)}, u32[]{:S(2)}, u32[]{:S(2)}) collective-permute-start(f32[2,128]{1,0:T(2,128)S(1)} %get-tuple-element.1801), channel_id=1, source_target_pairs={{8,0},{16,8},{24,16},{32,24},{40,32},{48,40},{56,48},{64,56},{72,6... | collective-permute-start | bytes 3080 | tf_op jit(solution)/shard_map/while/body/eval_jaxpr/ppermute | solution.py:17
  529.2 15.5 %collective-permute-start.6 = (bf16[128,256]{0,1:T(8,128)(2,1)S(1)}, bf16[128,256]{0,1:T(8,128)(2,1)S(1)}, u32[]{:S(2)}, u32[]{:S(2)}) collective-permute-start(bf16[128,256]{0,1:T(8,128)(2,1)S(1)} %get-tuple-element.1799), channel_id=1, source_target_pairs={{8,0},{16,8},{24,16},{32,24},{40,32},{48,40},{56,48},{64,56},{72,6... | collective-permute-start | bytes 196616 | tf_op jit(solution)/shard_map/while/body/eval_jaxpr/ppermute | solution.py:17
  531.1 11.2 %collective-permute-start.7 = (f32[2,128]{1,0:T(2,128)S(1)}, f32[2,128]{1,0:T(2,128)S(1)}, u32[]{:S(2)}, u32[]{:S(2)}) collective-permute-start(f32[2,128]{1,0:T(2,128)S(1)} %get-tuple-element.1801), channel_id=1, source_target_pairs={{8,0},{16,8},{24,16},{32,24},{40,32},{48,40},{56,48},{64,56},{72,6... | collective-permute-start | bytes 3080 | tf_op jit(solution)/shard_map/while/body/eval_jaxpr/ppermute | solution.py:17
  545.6 17.9 %collective-permute-start.6 = (bf16[128,256]{0,1:T(8,128)(2,1)S(1)}, bf16[128,256]{0,1:T(8,128)(2,1)S(1)}, u32[]{:S(2)}, u32[]{:S(2)}) collective-permute-start(bf16[128,256]{0,1:T(8,128)(2,1)S(1)} %get-tuple-element.1799), channel_id=1, source_target_pairs={{8,0},{16,8},{24,16},{32,24},{40,32},{48,40},{56,48},{64,56},{72,6... | collective-permute-start | bytes 196616 | tf_op jit(solution)/shard_map/while/body/eval_jaxpr/ppermute | solution.py:17
  547.5 13.6 %collective-permute-start.7 = (f32[2,128]{1,0:T(2,128)S(1)}, f32[2,128]{1,0:T(2,128)S(1)}, u32[]{:S(2)}, u32[]{:S(2)}) collective-permute-start(f32[2,128]{1,0:T(2,128)S(1)} %get-tuple-element.1801), channel_id=1, source_target_pairs={{8,0},{16,8},{24,16},{32,24},{40,32},{48,40},{56,48},{64,56},{72,6... | collective-permute-start | bytes 3080 | tf_op jit(solution)/shard_map/while/body/eval_jaxpr/ppermute | solution.py:17
  549.5 10.9 %collective-permute-start.8 = (s32[128]{0:T(128)S(1)}, s32[128]{0:T(128)S(1)}, u32[]{:S(2)}, u32[]{:S(2)}) collective-permute-start(s32[128]{0:T(128)S(1)} %get-tuple-element.1803), channel_id=1, source_target_pairs={{8,0},{16,8},{24,16},{32,24},{40,32},{48,40},{56,48},{64,56},{72,6... | collective-permute-start | bytes 1544 | tf_op jit(solution)/shard_map/while/body/eval_jaxpr/ppermute | solution.py:17
  553.5 10.3 %collective-permute-start.9 = (bf16[128,256]{0,1:T(8,128)(2,1)S(1)}, bf16[128,256]{0,1:T(8,128)(2,1)S(1)}, u32[]{:S(2)}, u32[]{:S(2)}) collective-permute-start(bf16[128,256]{0,1:T(8,128)(2,1)S(1)} %get-tuple-element.1800), channel_id=1, source_target_pairs={{8,0},{16,8},{24,16},{32,24},{40,32},{48,40},{56,48},{64,56},{72,6... | collective-permute-start | bytes 196616 | tf_op jit(solution)/shard_map/while/body/eval_jaxpr/ppermute | solution.py:17
  564.4 17.9 %collective-permute-start.6 = (bf16[128,256]{0,1:T(8,128)(2,1)S(1)}, bf16[128,256]{0,1:T(8,128)(2,1)S(1)}, u32[]{:S(2)}, u32[]{:S(2)}) collective-permute-start(bf16[128,256]{0,1:T(8,128)(2,1)S(1)} %get-tuple-element.1799), channel_id=1, source_target_pairs={{8,0},{16,8},{24,16},{32,24},{40,32},{48,40},{56,48},{64,56},{72,6... | collective-permute-start | bytes 196616 | tf_op jit(solution)/shard_map/while/body/eval_jaxpr/ppermute | solution.py:17
  566.4 13.6 %collective-permute-start.7 = (f32[2,128]{1,0:T(2,128)S(1)}, f32[2,128]{1,0:T(2,128)S(1)}, u32[]{:S(2)}, u32[]{:S(2)}) collective-permute-start(f32[2,128]{1,0:T(2,128)S(1)} %get-tuple-element.1801), channel_id=1, source_target_pairs={{8,0},{16,8},{24,16},{32,24},{40,32},{48,40},{56,48},{64,56},{72,6... | collective-permute-start | bytes 3080 | tf_op jit(solution)/shard_map/while/body/eval_jaxpr/ppermute | solution.py:17
  568.3 10.9 %collective-permute-start.8 = (s32[128]{0:T(128)S(1)}, s32[128]{0:T(128)S(1)}, u32[]{:S(2)}, u32[]{:S(2)}) collective-permute-start(s32[128]{0:T(128)S(1)} %get-tuple-element.1803), channel_id=1, source_target_pairs={{8,0},{16,8},{24,16},{32,24},{40,32},{48,40},{56,48},{64,56},{72,6... | collective-permute-start | bytes 1544 | tf_op jit(solution)/shard_map/while/body/eval_jaxpr/ppermute | solution.py:17
  572.3 10.3 %collective-permute-start.9 = (bf16[128,256]{0,1:T(8,128)(2,1)S(1)}, bf16[128,256]{0,1:T(8,128)(2,1)S(1)}, u32[]{:S(2)}, u32[]{:S(2)}) collective-permute-start(bf16[128,256]{0,1:T(8,128)(2,1)S(1)} %get-tuple-element.1800), channel_id=1, source_target_pairs={{8,0},{16,8},{24,16},{32,24},{40,32},{48,40},{56,48},{64,56},{72,6... | collective-permute-start | bytes 196616 | tf_op jit(solution)/shard_map/while/body/eval_jaxpr/ppermute | solution.py:17
  583.3 15.5 %collective-permute-start.6 = (bf16[128,256]{0,1:T(8,128)(2,1)S(1)}, bf16[128,256]{0,1:T(8,128)(2,1)S(1)}, u32[]{:S(2)}, u32[]{:S(2)}) collective-permute-start(bf16[128,256]{0,1:T(8,128)(2,1)S(1)} %get-tuple-element.1799), channel_id=1, source_target_pairs={{8,0},{16,8},{24,16},{32,24},{40,32},{48,40},{56,48},{64,56},{72,6... | collective-permute-start | bytes 196616 | tf_op jit(solution)/shard_map/while/body/eval_jaxpr/ppermute | solution.py:17
  585.2 11.2 %collective-permute-start.7 = (f32[2,128]{1,0:T(2,128)S(1)}, f32[2,128]{1,0:T(2,128)S(1)}, u32[]{:S(2)}, u32[]{:S(2)}) collective-permute-start(f32[2,128]{1,0:T(2,128)S(1)} %get-tuple-element.1801), channel_id=1, source_target_pairs={{8,0},{16,8},{24,16},{32,24},{40,32},{48,40},{56,48},{64,56},{72,6... | collective-permute-start | bytes 3080 | tf_op jit(solution)/shard_map/while/body/eval_jaxpr/ppermute | solution.py:17
  599.7 15.5 %collective-permute-start.6 = (bf16[128,256]{0,1:T(8,128)(2,1)S(1)}, bf16[128,256]{0,1:T(8,128)(2,1)S(1)}, u32[]{:S(2)}, u32[]{:S(2)}) collective-permute-start(bf16[128,256]{0,1:T(8,128)(2,1)S(1)} %get-tuple-element.1799), channel_id=1, source_target_pairs={{8,0},{16,8},{24,16},{32,24},{40,32},{48,40},{56,48},{64,56},{72,6... | collective-permute-start | bytes 196616 | tf_op jit(solution)/shard_map/while/body/eval_jaxpr/ppermute | solution.py:17
  601.6 11.2 %collective-permute-start.7 = (f32[2,128]{1,0:T(2,128)S(1)}, f32[2,128]{1,0:T(2,128)S(1)}, u32[]{:S(2)}, u32[]{:S(2)}) collective-permute-start(f32[2,128]{1,0:T(2,128)S(1)} %get-tuple-element.1801), channel_id=1, source_target_pairs={{8,0},{16,8},{24,16},{32,24},{40,32},{48,40},{56,48},{64,56},{72,6... | collective-permute-start | bytes 3080 | tf_op jit(solution)/shard_map/while/body/eval_jaxpr/ppermute | solution.py:17
  616.1 14.7 %collective-permute-start.6 = (bf16[128,256]{0,1:T(8,128)(2,1)S(1)}, bf16[128,256]{0,1:T(8,128)(2,1)S(1)}, u32[]{:S(2)}, u32[]{:S(2)}) collective-permute-start(bf16[128,256]{0,1:T(8,128)(2,1)S(1)} %get-tuple-element.1799), channel_id=1, source_target_pairs={{8,0},{16,8},{24,16},{32,24},{40,32},{48,40},{56,48},{64,56},{72,6... | collective-permute-start | bytes 196616 | tf_op jit(solution)/shard_map/while/body/eval_jaxpr/ppermute | solution.py:17
  618.1 10.4 %collective-permute-start.7 = (f32[2,128]{1,0:T(2,128)S(1)}, f32[2,128]{1,0:T(2,128)S(1)}, u32[]{:S(2)}, u32[]{:S(2)}) collective-permute-start(f32[2,128]{1,0:T(2,128)S(1)} %get-tuple-element.1801), channel_id=1, source_target_pairs={{8,0},{16,8},{24,16},{32,24},{40,32},{48,40},{56,48},{64,56},{72,6... | collective-permute-start | bytes 3080 | tf_op jit(solution)/shard_map/while/body/eval_jaxpr/ppermute | solution.py:17
  (120 other events, 916.6 us)
Sparse Core Ops, SparseCore 0:
  11.2 60.0 all-gather.1
where the time goes:
time: 645 us; the launch traced here: 640 us
  starting transfers between devices  491 us (76%)
  waiting for transfers between devices  38.6 us (6%)
  loops' own time  35.5 us (6%)
  matrix products  31.4 us (5%)
  other arithmetic  19.5 us (3%)
  between operations  15.5 us (2%)
  local copies, waits for them, and re-layouts  8.13 us (1%)
    ppermute x165, starting transfers between devices, shifted(): return lax.ppermute(block, axis, route)  491 us
    ppermute x165, waiting for transfers between devices, shifted(): return lax.ppermute(block, axis, route)  38.6 us
  transfers between devices with their start and end apart: 166, of which 43 were waited for; matrix products, arithmetic and copies ran while one was open for 6% of the time, Pallas kernels for 0%

commit v1 on v0

v1 whole, which is shorter than its diff:
```python
import functools

import jax
import jax.numpy as jnp
from jax import lax
from jax.experimental import pallas as pl
from jax.experimental.pallas import tpu as pltpu
from jax.sharding import PartitionSpec as P

MESH = pl.DeviceIdType.MESH
HEAD_DIM = 128
TILE = 128
SCALE = HEAD_DIM**-0.5
LOG2E = 1.4426950408889634
SCALE2 = SCALE * LOG2E
FAR_BELOW = -1.0e30
F32 = jnp.float32
BF16 = jnp.bfloat16


def nt(a, b):
    return lax.dot_general(a, b, (((1,), (1,)), ((), ())), preferred_element_type=F32)


def nn(a, b):
    return lax.dot_general(a, b, (((1,), (0,)), ((), ())), preferred_element_type=F32)


def kernel(
    q_hbm, k_hbm, v_hbm, doc_ref, frame_ref, x_hbm, w_hbm, out_ref,
    w, rows, kv_own, q_own, cot_own, kv, qb, cb, stats, stats_out, meta, scores,
    top, total, summed, dq, dk, dv, half_out, half_in, out_stage,
    load_sem, tp_send, tp_recv, kv_send, kv_pass, kv_recv, q_send, q_recv,
    c_send, c_recv, st_send, st_recv, meta_send, meta_recv, half_send, half_recv,
    out_send, out_recv,
):
    seq, tp = lax.axis_index("seq"), lax.axis_index("tp")
    plane = seq // 4
    first = (plane // 4) * 4
    z, y, c = plane % 4, (seq // 2) % 2, seq % 2
    x, hi = tp // 2, tp % 2
    far = 1 - hi

    def at(zz, yy, cc):
        return ((first + zz) * 4 + yy * 2 + cc, tp)

    def across(xx, hh):
        return (seq, ((xx + 4) % 4) * 2 + hh)

    def send(src, dst, send_sem, recv_sem, device):
        return pltpu.make_async_remote_copy(
            src_ref=src, dst_ref=dst, send_sem=send_sem, recv_sem=recv_sem,
            device_id=device, device_id_type=MESH,
        )

    mate = at(z, y, 1 - c)
    beside = at(z, 1 - y, c)
    x_up, x_down, x_far, y_far = across(x + 1, hi), across(x - 1, hi), across(x + 2, hi), across(x, far)

    barrier = pltpu.get_barrier_semaphore()
    for device in (x_up, x_down, x_far, y_far, mate):
        pl.semaphore_signal(barrier, inc=1, device_id=device, device_id_type=MESH)

    def greet(i, _):
        zz, yy = i // 2, i % 2

        @pl.when((zz != z) | (yy != y))
        def _():
            pl.semaphore_signal(barrier, inc=1, device_id=at(zz, yy, c), device_id_type=MESH)

        return 0

    lax.fori_loop(0, 8, greet, 0)

    def head(ref, h):
        return ref.at[:, pl.ds(h * HEAD_DIM, HEAD_DIM)]

    loads = [pltpu.make_async_copy(x_hbm, rows.at[hi, x], load_sem.at[0])]
    for h in range(2):
        loads.append(pltpu.make_async_copy(head(k_hbm, h), kv_own.at[h, 0], load_sem.at[1 + 3 * h]))
        loads.append(pltpu.make_async_copy(head(v_hbm, h), kv_own.at[h, 1], load_sem.at[2 + 3 * h]))
        loads.append(pltpu.make_async_copy(head(q_hbm, h), q_own.at[h], load_sem.at[3 + 3 * h]))
    load_w = pltpu.make_async_copy(w_hbm, w, load_sem.at[7])
    for load in loads:
        load.start()
    load_w.start()

    lane8 = lax.broadcasted_iota(jnp.int32, (8, 128), 0)
    begin = (doc_ref[0] - 1) * TILE - first * 512
    meta[y] = jnp.where(lane8 == 0, begin, frame_ref[0])

    for load in loads:
        load.wait()
    pl.semaphore_wait(barrier, 12)

    tp_first = [
        send(rows.at[hi, x], rows.at[hi, x], tp_send.at[i], tp_recv.at[i], device)
        for i, device in enumerate((x_up, x_down, x_far, y_far))
    ]
    for copy in tp_first:
        copy.start()

    def meta_copy():
        return send(meta.at[y], meta.at[y], meta_send, meta_recv, beside)

    def kv_copy(zz, h, device):
        return send(kv_own.at[h], kv.at[z, y, c], kv_send.at[zz, h], kv_recv.at[z, y, c], device)

    def q_copy(zz, h):
        return send(q_own.at[h], qb.at[z, y], q_send.at[zz, h], q_recv.at[z, y], at(zz, h, c))

    def c_copy(part, zz, h):
        return send(
            cot_own.at[h, :, part], cb.at[z, y, :, part], c_send.at[part, zz, h],
            c_recv.at[part, z, y], at(zz, h, c),
        )

    def all_kv(do):
        do(kv_copy(z, 1 - y, beside))
        do(kv_copy(z, y, mate))

        def step(zz, _):
            do(kv_copy(zz, y, at(zz, y, c)))
            do(kv_copy(zz, 1 - y, at(zz, 1 - y, c)))
            return 0

        lax.fori_loop(z + 1, 4, step, 0)

    def earlier(copy, do):
        do(copy(z, 1 - y))

        def step(i, _):
            zz = z - 1 - i
            do(copy(zz, y))
            do(copy(zz, 1 - y))
            return 0

        lax.fori_loop(0, z, step, 0)

    start = lambda copy: copy.start()
    sent = lambda copy: copy.wait_send()

    meta_copy().start()
    all_kv(start)
    earlier(q_copy, start)
    kv[z, y, c] = kv_own[y]
    qb[z, y] = q_own[y]

    def arrived_kv(zz, yy, cc):
        send(kv_own.at[0], kv.at[zz, yy, cc], kv_send.at[z, 0], kv_recv.at[zz, yy, cc], mate).wait_recv()

    def pass_kv(zz, yy):
        return send(kv.at[zz, yy, c], kv.at[zz, yy, c], kv_pass.at[zz, yy], kv_recv.at[zz, yy, c], mate)

    arrived_kv(z, 1 - y, c)
    pass_kv(z, 1 - y).start()

    tp_first[3].wait_recv()
    tp_second = [
        send(rows.at[far, x], rows.at[far, x], tp_send.at[4], tp_recv.at[4], x_up),
        send(rows.at[far, x], rows.at[far, x], tp_send.at[5], tp_recv.at[5], x_down),
    ]
    for copy in tp_second:
        copy.start()
    tp_first[2].wait_recv()
    x_other = (x + 2) % 4
    tp_second.append(
        send(rows.at[hi, x_other], rows.at[hi, x_other], tp_send.at[6], tp_recv.at[6], y_far)
    )
    tp_second[2].start()

    meta_copy().wait_recv()
    send(q_own.at[0], qb.at[z, y], q_send.at[z, 0], q_recv.at[z, 1 - y], mate).wait_recv()
    arrived_kv(z, y, 1 - c)
    arrived_kv(z, 1 - y, 1 - c)

    query = qb[z].reshape(256, HEAD_DIM)
    offset = lax.broadcasted_iota(jnp.int32, (128, 128), 0)
    low, high = [], []
    for tile in range(2):
        start_of = z * 512 + tile * 256 + c * 128
        low.append(jnp.broadcast_to(meta[tile][0:1], (128, 128)))
        framed = jnp.broadcast_to(meta[tile][1:2], (128, 128)) == 1
        high.append(jnp.where(framed, start_of + 127, start_of + offset))
    low = jnp.concatenate(low, axis=0)
    high = jnp.concatenate(high, axis=0)

    def keys_of(zz):
        return kv[zz, :, :, 0].reshape(512, HEAD_DIM)

    def values_of(zz):
        return kv[zz, :, :, 1].reshape(512, HEAD_DIM)

    def masked_scores(zz):
        place = zz * 512 + lax.broadcasted_iota(jnp.int32, (256, 512), 1)
        seen = (place >= low[:, :1]) & (place <= high[:, :1])
        return jnp.where(seen, nt(query, keys_of(zz)) * SCALE2, FAR_BELOW)

    s = masked_scores(z)
    scores[z] = s
    m = jnp.max(s, axis=1, keepdims=True)
    e = jnp.exp2(s - m)
    top[...] = jnp.broadcast_to(m, (256, 128))
    total[...] = jnp.broadcast_to(jnp.sum(e, axis=1, keepdims=True), (256, 128))
    summed[...] = nn(e.astype(BF16), values_of(z))

    def cotangent(part):
        block = nt(rows[part].reshape(64, -1), w[...]).astype(BF16)
        for h in range(2):
            cot_own[h, :, part] = block[:, h * 128 : (h + 1) * 128].reshape(4, 16, HEAD_DIM)
        cb[z, y, :, part] = cot_own[y, :, part]
        earlier(functools.partial(c_copy, part), start)

    tp_first[0].wait_recv()
    tp_first[1].wait_recv()
    load_w.wait()
    cotangent(hi)
    for copy in tp_second:
        copy.wait_recv()
    cotangent(far)

    def absorb(zz):
        s = masked_scores(zz)
        scores[zz] = s
        old = top[:, :1]
        m = jnp.maximum(old, jnp.max(s, axis=1, keepdims=True))
        e = jnp.exp2(s - m)
        factor = jnp.exp2(old - m)
        top[...] = jnp.broadcast_to(m, (256, 128))
        total[...] = total[...] * factor + jnp.sum(e, axis=1, keepdims=True)
        summed[...] = summed[...] * factor + nn(e.astype(BF16), values_of(zz))

    def forward_step(i, _):
        zz = z - 1 - i
        for yy in range(2):
            arrived_kv(zz, yy, c)
            pass_kv(zz, yy).start()
        for yy in range(2):
            arrived_kv(zz, yy, 1 - c)
        absorb(zz)
        return 0

    lax.fori_loop(0, z, forward_step, 0)

    attended = (summed[...] / total[...]).astype(BF16)
    log_total = top[...] + jnp.log2(total[...])

    def give(number, block):
        out_stage[number] = block.reshape(2, 128, HEAD_DIM)
        out_ref[number, y] = out_stage[number, y]
        out_copy(number).start()

    def out_copy(number):
        return send(
            out_stage.at[number, 1 - y], out_ref.at[number, y], out_send.at[number],
            out_recv.at[number], beside,
        )

    give(0, attended)

    def arrived_c(zz, yy):
        for part in range(2):
            send(
                cot_own.at[0, :, 0], cb.at[zz, yy, :, part], c_send.at[0, z, 0],
                c_recv.at[part, zz, yy], mate,
            ).wait_recv()

    arrived_c(z, 1 - y)
    own_cot = cb[z].reshape(256, HEAD_DIM)
    delta = jnp.sum(own_cot.astype(F32) * attended.astype(F32), axis=1, keepdims=True)
    lane = lax.broadcasted_iota(jnp.int32, (256, 128), 1)
    packed = jnp.where(
        lane == 0, log_total,
        jnp.where(lane == 1, delta, jnp.where(lane == 2, low.astype(F32), high.astype(F32))),
    )
    stats_out[...] = packed.T[:8]

    def st_copy(zz):
        return send(stats_out, stats.at[z], st_send.at[zz], st_recv.at[z], at(zz, y, c))

    def all_stats(do):
        def step(i, _):
            do(st_copy(z - 1 - i))
            return 0

        lax.fori_loop(0, z, step, 0)

    all_stats(start)
    stats[z] = stats_out[...]

    own_keys = keys_of(z)
    own_values = values_of(z)

    def key_side(zz):
        visit = qb[zz].reshape(256, HEAD_DIM)
        visit_cot = cb[zz].reshape(256, HEAD_DIM)
        rest = stats[zz]
        place = z * 512 + lax.broadcasted_iota(jnp.int32, (512, 256), 0)
        seen = (place >= rest[2:3].astype(jnp.int32)) & (place <= rest[3:4].astype(jnp.int32))
        s = jnp.where(seen, nt(own_keys, visit) * SCALE2, FAR_BELOW)
        p = jnp.exp2(s - rest[0:1])
        slopes = (p * (nt(own_values, visit_cot) - rest[1:2])).astype(BF16)
        return nn(slopes, visit), nn(p.astype(BF16), visit_cot)

    def query_side(zz):
        p = jnp.exp2(scores[zz] - log_total[:, :1])
        slopes = (p * (nt(own_cot, values_of(zz)) - delta)).astype(BF16)
        return nn(slopes, keys_of(zz))

    dk[...], dv[...] = key_side(z)
    dq[...] = query_side(z)

    def query_step(i, _):
        dq[...] += query_side(z - 1 - i)
        return 0

    lax.fori_loop(0, z, query_step, 0)
    give(1, (dq[...] * SCALE).astype(BF16))

    def key_step(zz, _):
        for yy in range(2):
            send(q_own.at[0], qb.at[zz, yy], q_send.at[z, 0], q_recv.at[zz, yy], mate).wait_recv()
            arrived_c(zz, yy)
        send(stats_out, stats.at[zz], st_send.at[z], st_recv.at[zz], mate).wait_recv()
        more_k, more_v = key_side(zz)
        dk[...] += more_k
        dv[...] += more_v
        return 0

    lax.fori_loop(z + 1, 4, key_step, 0)

    dk4 = dk.reshape(2, 2, 128, HEAD_DIM)
    dv4 = dv.reshape(2, 2, 128, HEAD_DIM)
    half_out[0] = dk4[:, 1 - c]
    half_out[1] = dv4[:, 1 - c]
    half = send(half_out, half_in, half_send, half_recv, mate)
    half.start()
    half.wait_recv()
    give(2, ((dk4[:, c] + half_in[0]) * SCALE).astype(BF16))
    give(3, (dv4[:, c] + half_in[1]).astype(BF16))

    for number in range(4):
        out_copy(number).wait_recv()

    for number in range(4):
        out_copy(number).wait_send()
    half.wait_send()
    for copy in tp_first + tp_second:
        copy.wait_send()
    meta_copy().wait_send()
    all_kv(sent)
    earlier(q_copy, sent)
    for part in range(2):
        earlier(functools.partial(c_copy, part), sent)
    all_stats(sent)
    pass_kv(z, 1 - y).wait_send()

    def passed(zz, _):
        for yy in range(2):
            pass_kv(zz, yy).wait_send()
        return 0

    lax.fori_loop(0, z, passed, 0)


def on_device(query, key, value, documents, frames, out_cotangent, output_weight):
    hbm = pl.BlockSpec(memory_space=pl.ANY)
    smem = pl.BlockSpec(memory_space=pltpu.SMEM)
    vmem = pltpu.VMEM
    dma = pltpu.SemaphoreType.DMA
    depth = out_cotangent.shape[1]
    out = pl.pallas_call(
        kernel,
        name="masked_attention",
        out_shape=jax.ShapeDtypeStruct((4, 2, 128, HEAD_DIM), BF16),
        in_specs=[hbm, hbm, hbm, smem, smem, hbm, hbm],
        out_specs=pl.BlockSpec(memory_space=vmem),
        scratch_shapes=[
            vmem((256, depth), BF16),
            vmem((2, 4, 16, depth), BF16),
            vmem((2, 2, 128, 128), BF16),
            vmem((2, 128, 128), BF16),
            vmem((2, 4, 2, 16, 128), BF16),
            vmem((4, 2, 2, 2, 128, 128), BF16),
            vmem((4, 2, 128, 128), BF16),
            vmem((4, 2, 4, 2, 16, 128), BF16),
            vmem((4, 8, 256), F32),
            vmem((8, 256), F32),
            vmem((2, 8, 128), jnp.int32),
            vmem((4, 256, 512), F32),
            vmem((256, 128), F32),
            vmem((256, 128), F32),
            vmem((256, 128), F32),
            vmem((256, 128), F32),
            vmem((512, 128), F32),
            vmem((512, 128), F32),
            vmem((2, 2, 128, 128), F32),
            vmem((2, 2, 128, 128), F32),
            vmem((4, 2, 128, 128), BF16),
            dma((8,)),
            dma((7,)), dma((7,)),
            dma((4, 2)), dma((4, 2)), dma((4, 2, 2)),
            dma((4, 2)), dma((4, 2)),
            dma((2, 4, 2)), dma((2, 4, 2)),
            dma((4,)), dma((4,)),
            dma, dma,
            dma, dma,
            dma((4,)), dma((4,)),
        ],
        compiler_params=pltpu.CompilerParams(
            collective_id=0, has_side_effects=True, vmem_limit_bytes=48 * 2**20
        ),
    )(query, key, value, documents, frames, out_cotangent, output_weight)
    return tuple(out[i].transpose(1, 0, 2).reshape(128, 256) for i in range(4))


def solution(mesh):
    whole = P("seq", "tp")
    return jax.shard_map(
        on_device,
        mesh=mesh,
        in_specs=(whole, whole, whole, P("seq"), P("seq"), P(("seq", "tp"), None), P("tp", None)),
        out_specs=(whole, whole, whole, whole),
        check_vma=False,
    )
```

time: 645 us -> 49.1 us (0.08)
  the two profiles are of different devices: /device:TPU:473 before, /device:TPU:1 now
where the time goes in v1:
time: 49.1 us; the launch traced here: 48.8 us
  Pallas kernels  38.3 us (78%)
  local copies, waits for them, and re-layouts  8.49 us (17%)
  between operations  1.98 us (4%)
    pallas_call x1, Pallas kernels, on_device(): pl.pallas_call(kernel, name='masked_attention', out_shape=jax.ShapeDtypeS...  38.3 us
    unnamed x14, local copies, waits for them, and re-layouts  8 us

profile of v1, /device:TPU:1, one launch (start us, length us, event | category | flops | bytes accessed | tf_op | source)
XLA Modules:
  0.0 48.8 jit_solution(10697508154727764146)
XLA Ops:
  1.9 0.0 copy-start
  1.9 1.6 %copy-done = bf16[256,4096]{1,0:T(8,128)(2,1)S(1)} copy-done((bf16[256,4096]{1,0:T(8,128)(2,1)S(1)}, bf16[256,4096]{1,0:T(8,128)(2,1)}, u32[]{:S(2)}) %copy-start) | copy-done | bytes 2097176
  3.5 0.0 copy-start.1
  3.5 0.9 %copy-done.1 = bf16[16,4096]{1,0:T(8,128)(2,1)S(1)} copy-done((bf16[16,4096]{1,0:T(8,128)(2,1)S(1)}, bf16[16,4096]{1,0:T(8,128)(2,1)}, u32[]{:S(2)}) %copy-start.1) | copy-done | bytes 131096
  4.4 0.0 copy-start.2
  4.4 0.8 %copy-done.2 = bf16[128,256]{1,0:T(8,128)(2,1)S(1)} copy-done((bf16[128,256]{1,0:T(8,128)(2,1)S(1)}, bf16[128,256]{1,0:T(8,128)(2,1)}, u32[]{:S(2)}) %copy-start.2) | copy-done | bytes 65560
  5.3 0.0 copy-start.3
  5.3 0.8 %copy-done.3 = bf16[128,256]{1,0:T(8,128)(2,1)S(1)} copy-done((bf16[128,256]{1,0:T(8,128)(2,1)S(1)}, bf16[128,256]{1,0:T(8,128)(2,1)}, u32[]{:S(2)}) %copy-start.3) | copy-done | bytes 65560
  6.1 0.0 copy-start.4
  6.1 0.8 %copy-done.4 = bf16[128,256]{1,0:T(8,128)(2,1)S(1)} copy-done((bf16[128,256]{1,0:T(8,128)(2,1)S(1)}, bf16[128,256]{1,0:T(8,128)(2,1)}, u32[]{:S(2)}) %copy-start.4) | copy-done | bytes 65560
  6.9 38.3 %masked_attention.1 = bf16[4,2,128,128]{3,2,1,0:T(8,128)(2,1)S(1)} custom-call(bf16[128,256]{1,0:T(8,128)(2,1)S(1)} %copy-done.2, bf16[128,256]{1,0:T(8,128)(2,1)S(1)} %copy-done.3, bf16[128,256]{1,0:T(8,128)(2,1)S(1)} %copy-done.4, s32[1]{0:T(128)S(6)} %copy.19.doc_ref, s32[1]{0:T(128)S(6)} %copy.20.frame_ref, bf16[16,4096]{1,0:T(8,128)(2,1)S(1)} %copy-done.1, ...), custom_call_target="tpu_custom_call" | custom-call | tf_op jit(solution)/shard_map/masked_attention/pallas_call | solution.py:372
  45.3 0.1 copy.14
  45.4 0.7 %copy.18 = bf16[128,256]{1,0:T(8,128)(2,1)} copy(bf16[128,256]{0,1:T(8,128)(2,1)S(1)} %bitcast.20) | data formatting | bytes 131072
  46.1 0.1 copy.13
  46.3 0.7 %copy.17 = bf16[128,256]{1,0:T(8,128)(2,1)} copy(bf16[128,256]{0,1:T(8,128)(2,1)S(1)} %bitcast.21) | data formatting | bytes 131072
  47.0 0.1 copy.12
  47.1 0.7 %copy.16 = bf16[128,256]{1,0:T(8,128)(2,1)} copy(bf16[128,256]{0,1:T(8,128)(2,1)S(1)} %bitcast.22) | data formatting | bytes 131072
  47.9 0.1 copy.11
  48.0 0.7 %copy.15 = bf16[128,256]{1,0:T(8,128)(2,1)} copy(bf16[128,256]{0,1:T(8,128)(2,1)S(1)} %bitcast.23) | data formatting | bytes 131072
  (1 shorter events, 0.0 us)
Async XLA Ops:
  1.9 1.6 %copy-start = (bf16[256,4096]{1,0:T(8,128)(2,1)S(1)}, bf16[256,4096]{1,0:T(8,128)(2,1)}, u32[]{:S(2)}) copy-start(bf16[256,4096]{1,0:T(8,128)(2,1)} %w_hbm.1) | copy-start | bytes 6291460
  3.5 0.9 %copy-start.1 = (bf16[16,4096]{1,0:T(8,128)(2,1)S(1)}, bf16[16,4096]{1,0:T(8,128)(2,1)}, u32[]{:S(2)}) copy-start(bf16[16,4096]{1,0:T(8,128)(2,1)} %x_hbm.1) | copy-start | bytes 393220
  4.4 0.8 %copy-start.2 = (bf16[128,256]{1,0:T(8,128)(2,1)S(1)}, bf16[128,256]{1,0:T(8,128)(2,1)}, u32[]{:S(2)}) copy-start(bf16[128,256]{1,0:T(8,128)(2,1)} %q_hbm.1) | copy-start | bytes 196612
  5.3 0.8 %copy-start.3 = (bf16[128,256]{1,0:T(8,128)(2,1)S(1)}, bf16[128,256]{1,0:T(8,128)(2,1)}, u32[]{:S(2)}) copy-start(bf16[128,256]{1,0:T(8,128)(2,1)} %k_hbm.1) | copy-start | bytes 196612
  6.1 0.8 %copy-start.4 = (bf16[128,256]{1,0:T(8,128)(2,1)S(1)}, bf16[128,256]{1,0:T(8,128)(2,1)}, u32[]{:S(2)}) copy-start(bf16[128,256]{1,0:T(8,128)(2,1)} %v_hbm.1) | copy-start | bytes 196612

commit v2 on v1

v2 whole, which is shorter than its diff:
```python
import contextlib
import functools

import jax
import jax.numpy as jnp
from jax import lax
from jax.experimental import pallas as pl
from jax.experimental.pallas import tpu as pltpu
from jax.sharding import PartitionSpec as P

MESH = pl.DeviceIdType.MESH
HEAD_DIM = 128
TILE = 128
SCALE = HEAD_DIM**-0.5
LOG2E = 1.4426950408889634
SCALE2 = SCALE * LOG2E
FAR_BELOW = -1.0e30
F32 = jnp.float32
BF16 = jnp.bfloat16
SCOPES = False


def scope(name):
    return jax.named_scope(name) if SCOPES else contextlib.nullcontext()


def nt(a, b):
    return lax.dot_general(a, b, (((1,), (1,)), ((), ())), preferred_element_type=F32)


def nn(a, b):
    return lax.dot_general(a, b, (((1,), (0,)), ((), ())), preferred_element_type=F32)


def kernel(
    q_hbm, k_hbm, v_hbm, doc_hbm, frame_hbm, x_hbm, w_hbm, out_ref,
    w, rows, kv_own, q_own, cot_own, kv, qb, cb, stats, stats_out, meta, scores,
    visits, top, total, summed, dq, dk, dv, half_out, half_in, out_stage,
    doc_ref, frame_ref, load_sem, tp_send, tp_recv, kv_send, kv_pass, kv_recv, q_send, q_recv,
    c_send, c_recv, st_send, st_recv, meta_send, meta_recv, half_send, half_recv,
    out_send, out_recv,
):
    seq, tp = lax.axis_index("seq"), lax.axis_index("tp")
    plane = seq // 4
    first = (plane // 4) * 4
    z, y, c = plane % 4, (seq // 2) % 2, seq % 2
    x, hi = tp // 2, tp % 2
    far = 1 - hi

    def at(zz, yy, cc):
        return ((first + zz) * 4 + yy * 2 + cc, tp)

    def across(xx, hh):
        return (seq, ((xx + 4) % 4) * 2 + hh)

    def send(src, dst, send_sem, recv_sem, device):
        return pltpu.make_async_remote_copy(
            src_ref=src, dst_ref=dst, send_sem=send_sem, recv_sem=recv_sem,
            device_id=device, device_id_type=MESH,
        )

    mate = at(z, y, 1 - c)
    beside = at(z, 1 - y, c)
    x_up, x_down, x_far, y_far = across(x + 1, hi), across(x - 1, hi), across(x + 2, hi), (
        at(z, 1 - y, c)[0], x * 2 + far
    )

    barrier = pltpu.get_barrier_semaphore()
    for device in (x_up, x_down, x_far, y_far, mate):
        pl.semaphore_signal(barrier, inc=1, device_id=device, device_id_type=MESH)

    def greet(i, _):
        zz, yy = i // 2, i % 2

        @pl.when((zz != z) | (yy != y))
        def _():
            pl.semaphore_signal(barrier, inc=1, device_id=at(zz, yy, c), device_id_type=MESH)

        return 0

    lax.fori_loop(0, 8, greet, 0)

    def head(ref, h):
        return ref.at[:, pl.ds(h * HEAD_DIM, HEAD_DIM)]

    loads = [pltpu.make_async_copy(x_hbm, rows.at[hi, x], load_sem.at[0])]
    for h in range(2):
        loads.append(pltpu.make_async_copy(head(k_hbm, h), kv_own.at[h, 0], load_sem.at[1 + 3 * h]))
        loads.append(pltpu.make_async_copy(head(v_hbm, h), kv_own.at[h, 1], load_sem.at[2 + 3 * h]))
        loads.append(pltpu.make_async_copy(head(q_hbm, h), q_own.at[h], load_sem.at[3 + 3 * h]))
    load_w = pltpu.make_async_copy(w_hbm, w, load_sem.at[7])
    for load in loads:
        load.start()
    load_w.start()
    marks = [
        pltpu.make_async_copy(doc_hbm, doc_ref, load_sem.at[8]),
        pltpu.make_async_copy(frame_hbm, frame_ref, load_sem.at[9]),
    ]
    for load in marks:
        load.start()
    for load in marks:
        load.wait()

    lane8 = lax.broadcasted_iota(jnp.int32, (8, 128), 0)
    begin = (doc_ref[0] - 1) * TILE - first * 512
    meta[y] = jnp.where(lane8 == 0, begin, frame_ref[0])

    with scope("load"):
        for load in loads:
            load.wait()
    with scope("barrier"):
        pl.semaphore_wait(barrier, 12)

    tp_first = [
        send(rows.at[hi, x], rows.at[hi, x], tp_send.at[i], tp_recv.at[i], device)
        for i, device in enumerate((x_up, x_down, x_far, y_far))
    ]
    with scope("tp_start"):
        for i in (3, 2, 0, 1):
            tp_first[i].start()

    def meta_copy():
        return send(meta.at[y], meta.at[y], meta_send, meta_recv, beside)

    def kv_copy(zz, h, device):
        return send(kv_own.at[h], kv.at[z, y, c], kv_send.at[zz, h], kv_recv.at[z, y, c], device)

    def q_copy(zz, h):
        return send(q_own.at[h], qb.at[z, y], q_send.at[zz, h], q_recv.at[z, y], at(zz, h, c))

    near_pair = pl.ds((x // 2) * 2, 2)
    far_pair = pl.ds(2 - (x // 2) * 2, 2)

    def part_of(ref, part):
        if part == 0:
            return ref.at[:, hi]
        return ref.at[near_pair if part == 1 else far_pair, far]

    def tile_of(part):
        return y if part == 0 else 1 - y

    def c_copy(part, zz, h):
        return send(
            part_of(cot_own.at[h], part), part_of(cb.at[z, tile_of(part)], part),
            c_send.at[part, zz, h], c_recv.at[part, z, tile_of(part)], at(zz, h, c),
        )

    def arrived_c(part, zz, yy):
        send(
            part_of(cot_own.at[0], part), part_of(cb.at[zz, yy], part), c_send.at[0, z, 0],
            c_recv.at[part, zz, yy], mate,
        ).wait_recv()

    def all_kv(do):
        do(kv_copy(z, 1 - y, beside))
        do(kv_copy(z, y, mate))

        def step(zz, _):
            do(kv_copy(zz, y, at(zz, y, c)))
            do(kv_copy(zz, 1 - y, at(zz, 1 - y, c)))
            return 0

        lax.fori_loop(z + 1, 4, step, 0)

    def earlier(copy, do):
        do(copy(z, 1 - y))
        below(copy, do)

    def below(copy, do):
        def step(i, _):
            do(copy(i, y))
            do(copy(i, 1 - y))
            return 0

        lax.fori_loop(0, z, step, 0)

    start = lambda copy: copy.start()
    sent = lambda copy: copy.wait_send()

    with scope("kvq_start"):
        meta_copy().start()
        all_kv(start)
        q_copy(z, 1 - y).start()
        kv[z, y, c] = kv_own[y]
        qb[z, y] = q_own[y]

    def arrived_kv(zz, yy, cc):
        send(kv_own.at[0], kv.at[zz, yy, cc], kv_send.at[z, 0], kv_recv.at[zz, yy, cc], mate).wait_recv()

    def pass_kv(zz, yy):
        return send(kv.at[zz, yy, c], kv.at[zz, yy, c], kv_pass.at[zz, yy], kv_recv.at[zz, yy, c], mate)

    with scope("kv_beside"):
        arrived_kv(z, 1 - y, c)
        pass_kv(z, 1 - y).start()

    with scope("tp_yfar"):
        tp_first[3].wait_recv()
    tp_second = [
        send(rows.at[far, x], rows.at[far, x], tp_send.at[4], tp_recv.at[4], x_up),
        send(rows.at[far, x], rows.at[far, x], tp_send.at[5], tp_recv.at[5], x_down),
    ]
    for copy in tp_second:
        copy.start()
    with scope("tp_xfar"):
        tp_first[2].wait_recv()
    x_other = (x + 2) % 4
    tp_second.append(
        send(rows.at[hi, x_other], rows.at[hi, x_other], tp_send.at[6], tp_recv.at[6], y_far)
    )
    tp_second[2].start()
    below(q_copy, start)

    with scope("own_group_wait"):
        meta_copy().wait_recv()
        send(q_own.at[0], qb.at[z, y], q_send.at[z, 0], q_recv.at[z, 1 - y], mate).wait_recv()
        arrived_kv(z, y, 1 - c)
        arrived_kv(z, 1 - y, 1 - c)

    query = qb[z].reshape(256, HEAD_DIM)
    offset = lax.broadcasted_iota(jnp.int32, (128, 128), 0)
    low, high = [], []
    for tile in range(2):
        start_of = z * 512 + tile * 256 + c * 128
        low.append(jnp.broadcast_to(meta[tile][0:1], (128, 128)))
        framed = jnp.broadcast_to(meta[tile][1:2], (128, 128)) == 1
        high.append(jnp.where(framed, start_of + 127, start_of + offset))
    low = jnp.concatenate(low, axis=0)
    high = jnp.concatenate(high, axis=0)

    def keys_of(zz):
        return kv[zz, :, :, 0].reshape(512, HEAD_DIM)

    def values_of(zz):
        return kv[zz, :, :, 1].reshape(512, HEAD_DIM)

    def masked_scores(zz):
        place = zz * 512 + lax.broadcasted_iota(jnp.int32, (256, 512), 1)
        seen = (place >= low[:, :1]) & (place <= high[:, :1])
        return jnp.where(seen, nt(query, keys_of(zz)) * SCALE2, FAR_BELOW)

    with scope("fwd_own_group"):
        s = masked_scores(z)
        scores[z] = s
        m = jnp.max(s, axis=1, keepdims=True)
        e = jnp.exp2(s - m)
        top[...] = jnp.broadcast_to(m, (256, 128))
        total[...] = jnp.broadcast_to(jnp.sum(e, axis=1, keepdims=True), (256, 128))
        summed[...] = nn(e.astype(BF16), values_of(z))

    def cotangent(part):
        if part == 0:
            picked, count = rows[hi], 4
        else:
            picked, count = rows[far, near_pair if part == 1 else far_pair], 2
        block = nt(picked.reshape(count * 16, -1), w[...]).astype(BF16)
        for h in range(2):
            mine = block[:, h * 128 : (h + 1) * 128].reshape(count, 16, HEAD_DIM)
            if part == 0:
                cot_own[h, :, hi] = mine
            else:
                cot_own[h, near_pair if part == 1 else far_pair, far] = mine
        if part == 0:
            cb[z, y, :, hi] = cot_own[y, :, hi]
        else:
            pair = near_pair if part == 1 else far_pair
            cb[z, 1 - y, pair, far] = cot_own[y, pair, far]
        earlier(functools.partial(c_copy, part), start)

    with scope("tp_near_wait"):
        tp_first[0].wait_recv()
        tp_first[1].wait_recv()
        load_w.wait()
    with scope("cot_near"):
        cotangent(0)

    def arrived_far(xx, number):
        send(rows.at[far, xx], rows.at[far, xx], tp_send.at[4], tp_recv.at[number], x_up).wait_recv()

    odd = x % 2
    with scope("tp_far_wait"):
        arrived_far(x + 1 - 2 * odd, 5 - odd)
    with scope("cot_far_1"):
        cotangent(1)
    with scope("tp_far_wait"):
        arrived_far((x + 3 + 2 * odd) % 4, 4 + odd)
        tp_second[2].wait_recv()
    with scope("cot_far_2"):
        cotangent(2)

    def absorb(zz):
        s = masked_scores(zz)
        scores[zz] = s
        old = top[:, :1]
        m = jnp.maximum(old, jnp.max(s, axis=1, keepdims=True))
        e = jnp.exp2(s - m)
        factor = jnp.exp2(old - m)
        top[...] = jnp.broadcast_to(m, (256, 128))
        total[...] = total[...] * factor + jnp.sum(e, axis=1, keepdims=True)
        summed[...] = summed[...] * factor + nn(e.astype(BF16), values_of(zz))

    def pass_step(i, _):
        zz = z - 1 - i
        with scope("kv_wait"):
            for yy in range(2):
                arrived_kv(zz, yy, c)
                pass_kv(zz, yy).start()
        return 0

    lax.fori_loop(0, z, pass_step, 0)

    def forward_step(i, _):
        zz = z - 1 - i
        with scope("absorb"):
            for yy in range(2):
                arrived_kv(zz, yy, 1 - c)
            absorb(zz)
        return 0

    lax.fori_loop(0, z, forward_step, 0)

    with scope("normalise"):
        attended = (summed[...] / total[...]).astype(BF16)
        log_total = top[...] + jnp.log2(total[...])

    def give(number, block):
        out_stage[number] = block.reshape(2, 128, HEAD_DIM)
        out_copy(number).start()
        out_keep(number).start()

    def out_keep(number):
        return pltpu.make_async_copy(
            out_stage.at[number, y], out_ref.at[number, y], load_sem.at[number]
        )

    def out_copy(number):
        return send(
            out_stage.at[number, 1 - y], out_ref.at[number, y], out_send.at[number],
            out_recv.at[number], beside,
        )

    give(0, attended)

    with scope("own_cot_wait"):
        arrived_c(0, z, 1 - y)
        arrived_c(1, z, y)
        arrived_c(2, z, y)
    with scope("delta"):
        own_cot = cb[z].reshape(256, HEAD_DIM)
        delta = jnp.sum(own_cot.astype(F32) * attended.astype(F32), axis=1, keepdims=True)
        lane = lax.broadcasted_iota(jnp.int32, (256, 128), 1)
        packed = jnp.where(
            lane == 0, log_total,
            jnp.where(lane == 1, delta, jnp.where(lane == 2, low.astype(F32), high.astype(F32))),
        )
        stats_out[...] = packed.T[:8]

    def st_copy(zz):
        return send(stats_out, stats.at[z], st_send.at[zz], st_recv.at[z], at(zz, y, c))

    def all_stats(do):
        def step(i, _):
            do(st_copy(z - 1 - i))
            return 0

        lax.fori_loop(0, z, step, 0)

    all_stats(start)
    stats[z] = stats_out[...]

    own_keys = keys_of(z)
    own_values = values_of(z)

    def key_side(zz):
        visit = qb[zz].reshape(256, HEAD_DIM)
        visit_cot = cb[zz].reshape(256, HEAD_DIM)
        rest = stats[zz]
        place = z * 512 + lax.broadcasted_iota(jnp.int32, (512, 256), 0)
        seen = (place >= rest[2:3].astype(jnp.int32)) & (place <= rest[3:4].astype(jnp.int32))
        s = jnp.where(seen, visits[zz] * SCALE2, FAR_BELOW)
        p = jnp.exp2(s - rest[0:1])
        slopes = (p * (nt(own_values, visit_cot) - rest[1:2])).astype(BF16)
        return nn(slopes, visit), nn(p.astype(BF16), visit_cot)

    def query_side(zz):
        p = jnp.exp2(scores[zz] - log_total[:, :1])
        slopes = (p * (nt(own_cot, values_of(zz)) - delta)).astype(BF16)
        return nn(slopes, keys_of(zz))

    visits[z] = nt(own_keys, query)
    with scope("key_side_own"):
        dk[...], dv[...] = key_side(z)
    with scope("query_side_own"):
        dq[...] = query_side(z)

    def query_step(i, _):
        with scope("query_side"):
            dq[...] += query_side(z - 1 - i)
        return 0

    lax.fori_loop(0, z, query_step, 0)
    give(1, (dq[...] * SCALE).astype(BF16))

    def arrived_q(zz, yy):
        send(q_own.at[0], qb.at[zz, yy], q_send.at[z, 0], q_recv.at[zz, yy], mate).wait_recv()

    def ahead(zz, _):
        arrived_q(zz, 0)
        arrived_q(zz, 1)
        visits[zz] = nt(own_keys, qb[zz].reshape(256, HEAD_DIM))
        return 0

    lax.fori_loop(z + 1, 4, ahead, 0)

    for copy in tp_first + tp_second:
        copy.wait_send()
    meta_copy().wait_send()
    all_kv(sent)
    earlier(q_copy, sent)
    for part in range(3):
        earlier(functools.partial(c_copy, part), sent)
    all_stats(sent)
    pass_kv(z, 1 - y).wait_send()

    def passed(zz, _):
        for yy in range(2):
            pass_kv(zz, yy).wait_send()
        return 0

    lax.fori_loop(0, z, passed, 0)

    def key_step(zz, _):
        with scope("qc_wait"):
            for yy in range(2):
                for part in range(3):
                    arrived_c(part, zz, yy)
        with scope("stats_wait"):
            send(stats_out, stats.at[zz], st_send.at[z], st_recv.at[zz], mate).wait_recv()
        with scope("key_side"):
            more_k, more_v = key_side(zz)
            dk[...] += more_k
            dv[...] += more_v
        return 0

    lax.fori_loop(z + 1, 4, key_step, 0)

    dk4 = dk.reshape(2, 2, 128, HEAD_DIM)
    dv4 = dv.reshape(2, 2, 128, HEAD_DIM)
    with scope("halves"):
        half_out[0] = dk4[:, 1 - c].astype(BF16)
        half_out[1] = dv4[:, 1 - c].astype(BF16)
        half = send(half_out, half_in, half_send, half_recv, mate)
        half.start()
        half.wait_recv()
    with scope("give_kv"):
        give(2, ((dk4[:, c] + half_in[0]) * SCALE).astype(BF16))
        give(3, (dv4[:, c] + half_in[1]).astype(BF16))

    with scope("out_wait"):
        for number in range(4):
            out_keep(number).wait()
            out_copy(number).wait_recv()

    for number in range(4):
        out_copy(number).wait_send()
    half.wait_send()


def spread_kernel(blocks, *refs):
    outs, sem = refs[:4], refs[4]
    copies = [
        pltpu.make_async_copy(
            blocks.at[i, h], outs[i].at[:, pl.ds(h * HEAD_DIM, HEAD_DIM)], sem.at[i, h]
        )
        for i in range(4)
        for h in range(2)
    ]
    for copy in copies:
        copy.start()
    for copy in copies:
        copy.wait()


def on_device(query, key, value, documents, frames, out_cotangent, output_weight):
    hbm = pl.BlockSpec(memory_space=pltpu.HBM)
    vmem = pltpu.VMEM
    dma = pltpu.SemaphoreType.DMA
    depth = out_cotangent.shape[1]
    out = pl.pallas_call(
        kernel,
        name="masked_attention",
        out_shape=pltpu.VMEM((4, 2, 128, HEAD_DIM), BF16),
        in_specs=[hbm] * 7,
        out_specs=pl.BlockSpec(memory_space=vmem),
        scratch_shapes=[
            vmem((256, depth), BF16),
            vmem((2, 4, 16, depth), BF16),
            vmem((2, 2, 128, 128), BF16),
            vmem((2, 128, 128), BF16),
            vmem((2, 4, 2, 16, 128), BF16),
            vmem((4, 2, 2, 2, 128, 128), BF16),
            vmem((4, 2, 128, 128), BF16),
            vmem((4, 2, 4, 2, 16, 128), BF16),
            vmem((4, 8, 256), F32),
            vmem((8, 256), F32),
            vmem((2, 8, 128), jnp.int32),
            vmem((4, 256, 512), F32),
            vmem((4, 512, 256), F32),
            vmem((256, 128), F32),
            vmem((256, 128), F32),
            vmem((256, 128), F32),
            vmem((256, 128), F32),
            vmem((512, 128), F32),
            vmem((512, 128), F32),
            vmem((2, 2, 128, 128), BF16),
            vmem((2, 2, 128, 128), BF16),
            vmem((4, 2, 128, 128), BF16),
            pltpu.SMEM((1,), jnp.int32), pltpu.SMEM((1,), jnp.int32),
            dma((10,)),
            dma((7,)), dma((7,)),
            dma((4, 2)), dma((4, 2)), dma((4, 2, 2)),
            dma((4, 2)), dma((4, 2)),
            dma((3, 4, 2)), dma((3, 4, 2)),
            dma((4,)), dma((4,)),
            dma, dma,
            dma, dma,
            dma((4,)), dma((4,)),
        ],
        compiler_params=pltpu.CompilerParams(
            collective_id=0, has_side_effects=True, vmem_limit_bytes=62 * 2**20
        ),
    )(query, key, value, documents, frames, out_cotangent, output_weight)
    return pl.pallas_call(
        spread_kernel,
        name="spread_heads",
        out_shape=[jax.ShapeDtypeStruct((128, 256), BF16)] * 4,
        in_specs=[pl.BlockSpec(memory_space=vmem)],
        out_specs=[hbm] * 4,
        scratch_shapes=[dma((4, 2))],
        compiler_params=pltpu.CompilerParams(vmem_limit_bytes=40 * 2**20),
    )(out)


def solution(mesh):
    whole = P("seq", "tp")
    return jax.shard_map(
        on_device,
        mesh=mesh,
        in_specs=(whole, whole, whole, P("seq"), P("seq"), P(("seq", "tp"), None), P("tp", None)),
        out_specs=(whole, whole, whole, whole),
        check_vma=False,
    )
```

time: 49.1 us -> 35.5 us (0.72)
  local copies, waits for them, and re-layouts: 8.49 us -> 0 us
  Pallas kernels: 38.3 us -> 33.4 us
    unnamed x14 -> x0, local copies, waits for them, and re-layouts: 8 us -> none
    pallas_call x1 -> x2, Pallas kernels: 38.3 us -> 33.4 us  [the longest x1 32.7 us: on_device(): pl.pallas_call(kernel, name='masked_attention', out_shape=pltpu.VMEM((4,...]
    transpose x5 -> x0, local copies, waits for them, and re-layouts: 0.49 us -> none  [on_device(): out[i].transpose(1, 0, 2).reshape(128, 256)]
where the time goes in v2:
time: 35.5 us; the launch traced here: 35.4 us
  Pallas kernels  33.4 us (94%)
  between operations  1.93 us (5%)
    pallas_call x1, Pallas kernels, on_device(): pl.pallas_call(kernel, name='masked_attention', out_shape=pltpu.VMEM((4,...  32.7 us
    pallas_call x1, Pallas kernels, on_device(): pl.pallas_call(spread_kernel, name='spread_heads', out_shape=[jax.ShapeDt...  0.76 us

profile of v2, /device:TPU:1, one launch (start us, length us, event | category | flops | bytes accessed | tf_op | source)
XLA Modules:
  0.0 35.4 jit_solution(9091437980188209364)
XLA Ops:
  1.9 32.7 %masked_attention.1.blocks = bf16[4,2,128,128]{3,2,1,0:T(8,128)(2,1)S(1)} custom-call(bf16[128,256]{1,0:T(8,128)(2,1)} %q_hbm.1, bf16[128,256]{1,0:T(8,128)(2,1)} %k_hbm.1, bf16[128,256]{1,0:T(8,128)(2,1)} %v_hbm.1, s32[1]{0:T(128)S(6)} %copy.11.doc_hbm, s32[1]{0:T(128)S(6)} %copy.12.frame_hbm, bf16[16,4096]{1,0:T(8,128)(2,1)} %x_hbm.1, bf16[256,4096]{1,0:T(8,128)(2,1)} %w_hbm.1), custom_call_target="tpu_custom_call" | custom-call | tf_op jit(solution)/shard_map/masked_attention/pallas_call | solution.py:489
  34.6 0.8 %spread_heads.1 = (bf16[128,256]{1,0:T(8,128)(2,1)}, bf16[128,256]{1,0:T(8,128)(2,1)}, bf16[128,256]{1,0:T(8,128)(2,1)}, bf16[128,256]{1,0:T(8,128)(2,1)}) custom-call(bf16[4,2,128,128]{3,2,1,0:T(8,128)(2,1)S(1)} %masked_attention.1.blocks), custom_call_target="tpu_custom_call" | custom-call | tf_op jit(solution)/shard_map/spread_heads/pallas_call | solution.py:533

commit v3 on v2

--- a/solution.py
+++ b/solution.py
@@ -34,9 +34,9 @@
 
 def kernel(
     q_hbm, k_hbm, v_hbm, doc_hbm, frame_hbm, x_hbm, w_hbm, out_ref,
-    w, rows, kv_own, q_own, cot_own, kv, qb, cb, stats, stats_out, meta, scores,
+    w, wt, rows, kv_own, q_own, cot_own, kv, qb, cb, stats, stats_out, meta, scores,
     visits, top, total, summed, dq, dk, dv, half_out, half_in, out_stage,
-    doc_ref, frame_ref, load_sem, tp_send, tp_recv, kv_send, kv_pass, kv_recv, q_send, q_recv,
+    doc_ref, frame_ref, load_sem, tp_send, tp_recv, kv_send, kv_pass, kv_relay, kv_recv, q_send, q_recv,
     c_send, c_recv, st_send, st_recv, meta_send, meta_recv, half_send, half_recv,
     out_send, out_recv,
 ):
@@ -128,13 +128,8 @@
     def q_copy(zz, h):
         return send(q_own.at[h], qb.at[z, y], q_send.at[zz, h], q_recv.at[z, y], at(zz, h, c))
 
-    near_pair = pl.ds((x // 2) * 2, 2)
-    far_pair = pl.ds(2 - (x // 2) * 2, 2)
-
     def part_of(ref, part):
-        if part == 0:
-            return ref.at[:, hi]
-        return ref.at[near_pair if part == 1 else far_pair, far]
+        return ref.at[:, hi if part == 0 else far]
 
     def tile_of(part):
         return y if part == 0 else 1 - y
@@ -160,7 +155,7 @@
             do(kv_copy(zz, 1 - y, at(zz, 1 - y, c)))
             return 0
 
-        lax.fori_loop(z + 1, 4, step, 0)
+        lax.fori_loop(z + 1, 3 + (z + 3) // 4, step, 0)
 
     def earlier(copy, do):
         do(copy(z, 1 - y))
@@ -181,6 +176,7 @@
         meta_copy().start()
         all_kv(start)
         q_copy(z, 1 - y).start()
+        below(q_copy, start)
         kv[z, y, c] = kv_own[y]
         qb[z, y] = q_own[y]
 
@@ -190,9 +186,14 @@
     def pass_kv(zz, yy):
         return send(kv.at[zz, yy, c], kv.at[zz, yy, c], kv_pass.at[zz, yy], kv_recv.at[zz, yy, c], mate)
 
-    with scope("kv_beside"):
-        arrived_kv(z, 1 - y, c)
-        pass_kv(z, 1 - y).start()
+    load_w.wait()
+
+    def turn(i, _):
+        here = pl.ds(pl.multiple_of(i * 256, 256), 256)
+        wt[here, :] = w[:, here].T
+        return 0
+
+    lax.fori_loop(0, w.shape[1] // 256, turn, 0)
 
     with scope("tp_yfar"):
         tp_first[3].wait_recv()
@@ -209,7 +210,21 @@
         send(rows.at[hi, x_other], rows.at[hi, x_other], tp_send.at[6], tp_recv.at[6], y_far)
     )
     tp_second[2].start()
-    below(q_copy, start)
+    with scope("kv_beside"):
+        arrived_kv(z, 1 - y, c)
+        pass_kv(z, 1 - y).start()
+
+
+    def relay(yy):
+        return send(kv.at[0, yy, c], kv.at[0, yy, c], kv_relay.at[yy], kv_recv.at[0, yy, c], at(3, y, c))
+
+    @pl.when(z == 2)
+    def _():
+        with scope("relay"):
+            for yy in range(2):
+                arrived_kv(0, yy, c)
+                relay(yy).start()
+                pass_kv(0, yy).start()
 
     with scope("own_group_wait"):
         meta_copy().wait_recv()
@@ -248,46 +263,6 @@
         total[...] = jnp.broadcast_to(jnp.sum(e, axis=1, keepdims=True), (256, 128))
         summed[...] = nn(e.astype(BF16), values_of(z))
 
-    def cotangent(part):
-        if part == 0:
-            picked, count = rows[hi], 4
-        else:
-            picked, count = rows[far, near_pair if part == 1 else far_pair], 2
-        block = nt(picked.reshape(count * 16, -1), w[...]).astype(BF16)
-        for h in range(2):
-            mine = block[:, h * 128 : (h + 1) * 128].reshape(count, 16, HEAD_DIM)
-            if part == 0:
-                cot_own[h, :, hi] = mine
-            else:
-                cot_own[h, near_pair if part == 1 else far_pair, far] = mine
-        if part == 0:
-            cb[z, y, :, hi] = cot_own[y, :, hi]
-        else:
-            pair = near_pair if part == 1 else far_pair
-            cb[z, 1 - y, pair, far] = cot_own[y, pair, far]
-        earlier(functools.partial(c_copy, part), start)
-
-    with scope("tp_near_wait"):
-        tp_first[0].wait_recv()
-        tp_first[1].wait_recv()
-        load_w.wait()
-    with scope("cot_near"):
-        cotangent(0)
-
-    def arrived_far(xx, number):
-        send(rows.at[far, xx], rows.at[far, xx], tp_send.at[4], tp_recv.at[number], x_up).wait_recv()
-
-    odd = x % 2
-    with scope("tp_far_wait"):
-        arrived_far(x + 1 - 2 * odd, 5 - odd)
-    with scope("cot_far_1"):
-        cotangent(1)
-    with scope("tp_far_wait"):
-        arrived_far((x + 3 + 2 * odd) % 4, 4 + odd)
-        tp_second[2].wait_recv()
-    with scope("cot_far_2"):
-        cotangent(2)
-
     def absorb(zz):
         s = masked_scores(zz)
         scores[zz] = s
@@ -299,15 +274,54 @@
         total[...] = total[...] * factor + jnp.sum(e, axis=1, keepdims=True)
         summed[...] = summed[...] * factor + nn(e.astype(BF16), values_of(zz))
 
-    def pass_step(i, _):
+    def take(zz):
+        for yy in range(2):
+            arrived_kv(zz, yy, c)
+            pass_kv(zz, yy).start()
+
+    def cotangent(part):
+        half = hi if part == 0 else far
+        block = nn(rows[half].reshape(64, -1), wt[...]).astype(BF16)
+        for h in range(2):
+            cot_own[h, :, half] = block[:, h * 128 : (h + 1) * 128].reshape(4, 16, HEAD_DIM)
+        cb[z, tile_of(part), :, half] = cot_own[y, :, half]
+        earlier(functools.partial(c_copy, part), start)
+
+    with scope("tp_near_wait"):
+        tp_first[0].wait_recv()
+        tp_first[1].wait_recv()
+    with scope("cot_near"):
+        cotangent(0)
+
+    @pl.when(z > 0)
+    def _():
+        with scope("kv_wait"):
+            take(z - 1)
+
+    @pl.when(z > 0)
+    def _():
+        with scope("absorb"):
+            for yy in range(2):
+                arrived_kv(z - 1, yy, 1 - c)
+            absorb(z - 1)
+
+    with scope("tp_far_wait"):
+        for copy in tp_second:
+            copy.wait_recv()
+    with scope("cot_far"):
+        cotangent(1)
+
+    def take_step(i, _):
         zz = z - 1 - i
         with scope("kv_wait"):
-            for yy in range(2):
-                arrived_kv(zz, yy, c)
-                pass_kv(zz, yy).start()
-        return 0
-
-    lax.fori_loop(0, z, pass_step, 0)
+
+            @pl.when(z != 2)
+            def _():
+                take(zz)
+
+        return 0
+
+    lax.fori_loop(1, z, take_step, 0)
 
     def forward_step(i, _):
         zz = z - 1 - i
@@ -317,7 +331,7 @@
             absorb(zz)
         return 0
 
-    lax.fori_loop(0, z, forward_step, 0)
+    lax.fori_loop(1, z, forward_step, 0)
 
     with scope("normalise"):
         attended = (summed[...] / total[...]).astype(BF16)
@@ -344,7 +358,6 @@
     with scope("own_cot_wait"):
         arrived_c(0, z, 1 - y)
         arrived_c(1, z, y)
-        arrived_c(2, z, y)
     with scope("delta"):
         own_cot = cb[z].reshape(256, HEAD_DIM)
         delta = jnp.sum(own_cot.astype(F32) * attended.astype(F32), axis=1, keepdims=True)
@@ -417,11 +430,16 @@
     meta_copy().wait_send()
     all_kv(sent)
     earlier(q_copy, sent)
-    for part in range(3):
+    for part in range(2):
         earlier(functools.partial(c_copy, part), sent)
     all_stats(sent)
     pass_kv(z, 1 - y).wait_send()
 
+    @pl.when(z == 2)
+    def _():
+        for yy in range(2):
+            relay(yy).wait_send()
+
     def passed(zz, _):
         for yy in range(2):
             pass_kv(zz, yy).wait_send()
@@ -432,7 +450,7 @@
     def key_step(zz, _):
         with scope("qc_wait"):
             for yy in range(2):
-                for part in range(3):
+                for part in range(2):
                     arrived_c(part, zz, yy)
         with scope("stats_wait"):
             send(stats_out, stats.at[zz], st_send.at[z], st_recv.at[zz], mate).wait_recv()
@@ -494,6 +512,7 @@
         out_specs=pl.BlockSpec(memory_space=vmem),
         scratch_shapes=[
             vmem((256, depth), BF16),
+            vmem((depth, 256), BF16),
             vmem((2, 4, 16, depth), BF16),
             vmem((2, 2, 128, 128), BF16),
             vmem((2, 128, 128), BF16),
@@ -518,9 +537,9 @@
             pltpu.SMEM((1,), jnp.int32), pltpu.SMEM((1,), jnp.int32),
             dma((10,)),
             dma((7,)), dma((7,)),
-            dma((4, 2)), dma((4, 2)), dma((4, 2, 2)),
+            dma((4, 2)), dma((4, 2)), dma((2,)), dma((4, 2, 2)),
             dma((4, 2)), dma((4, 2)),
-            dma((3, 4, 2)), dma((3, 4, 2)),
+            dma((2, 4, 2)), dma((2, 4, 2)),
             dma((4,)), dma((4,)),
             dma, dma,
             dma, dma,

time: 35.5 us -> 34.7 us (0.977)
  Pallas kernels: 33.4 us -> 32.6 us
    pallas_call x1, Pallas kernels: 32.7 us -> 31.8 us  [on_device(): pl.pallas_call(kernel, name='masked_attention', out_shape=pltpu.VMEM((4,...]
where the time goes in v3:
time: 34.7 us; the launch traced here: 34.5 us
  Pallas kernels  32.6 us (94%)
  between operations  1.93 us (6%)
    pallas_call x1, Pallas kernels, on_device(): pl.pallas_call(kernel, name='masked_attention', out_shape=pltpu.VMEM((4,...  31.8 us
    pallas_call x1, Pallas kernels, on_device(): pl.pallas_call(spread_kernel, name='spread_heads', out_shape=[jax.ShapeDt...  0.76 us

profile of v3, /device:TPU:1, one launch (start us, length us, event | category | flops | bytes accessed | tf_op | source)
XLA Modules:
  0.0 34.5 jit_solution(11232136116276519428)
XLA Ops:
  1.9 31.8 %masked_attention.1.blocks = bf16[4,2,128,128]{3,2,1,0:T(8,128)(2,1)S(1)} custom-call(bf16[128,256]{1,0:T(8,128)(2,1)} %q_hbm.1, bf16[128,256]{1,0:T(8,128)(2,1)} %k_hbm.1, bf16[128,256]{1,0:T(8,128)(2,1)} %v_hbm.1, s32[1]{0:T(128)S(6)} %copy.11.doc_hbm, s32[1]{0:T(128)S(6)} %copy.12.frame_hbm, bf16[16,4096]{1,0:T(8,128)(2,1)} %x_hbm.1, bf16[256,4096]{1,0:T(8,128)(2,1)} %w_hbm.1), custom_call_target="tpu_custom_call" | custom-call | tf_op jit(solution)/shard_map/masked_attention/pallas_call | solution.py:507
  33.7 0.8 %spread_heads.1 = (bf16[128,256]{1,0:T(8,128)(2,1)}, bf16[128,256]{1,0:T(8,128)(2,1)}, bf16[128,256]{1,0:T(8,128)(2,1)}, bf16[128,256]{1,0:T(8,128)(2,1)}) custom-call(bf16[4,2,128,128]{3,2,1,0:T(8,128)(2,1)S(1)} %masked_attention.1.blocks), custom_call_target="tpu_custom_call" | custom-call | tf_op jit(solution)/shard_map/spread_heads/pallas_call | solution.py:552

commit v4 on v3

--- a/solution.py
+++ b/solution.py
@@ -35,9 +35,9 @@
 def kernel(
     q_hbm, k_hbm, v_hbm, doc_hbm, frame_hbm, x_hbm, w_hbm, out_ref,
     w, wt, rows, kv_own, q_own, cot_own, kv, qb, cb, stats, stats_out, meta, scores,
-    visits, top, total, summed, dq, dk, dv, half_out, half_in, out_stage,
+    visits, top, total, summed, dq, dk, dv, shares, got, out_stage,
     doc_ref, frame_ref, load_sem, tp_send, tp_recv, kv_send, kv_pass, kv_relay, kv_recv, q_send, q_recv,
-    c_send, c_recv, st_send, st_recv, meta_send, meta_recv, half_send, half_recv,
+    c_send, c_recv, st_send, st_recv, meta_send, meta_recv, share_send, share_recv,
     out_send, out_recv,
 ):
     seq, tp = lax.axis_index("seq"), lax.axis_index("tp")
@@ -66,7 +66,7 @@
     )
 
     barrier = pltpu.get_barrier_semaphore()
-    for device in (x_up, x_down, x_far, y_far, mate):
+    for device in (x_up, x_down, x_far, y_far, mate, at(z, 1 - y, 1 - c)):
         pl.semaphore_signal(barrier, inc=1, device_id=device, device_id_type=MESH)
 
     def greet(i, _):
@@ -109,7 +109,7 @@
         for load in loads:
             load.wait()
     with scope("barrier"):
-        pl.semaphore_wait(barrier, 12)
+        pl.semaphore_wait(barrier, 13)
 
     tp_first = [
         send(rows.at[hi, x], rows.at[hi, x], tp_send.at[i], tp_recv.at[i], device)
@@ -390,7 +390,7 @@
         rest = stats[zz]
         place = z * 512 + lax.broadcasted_iota(jnp.int32, (512, 256), 0)
         seen = (place >= rest[2:3].astype(jnp.int32)) & (place <= rest[3:4].astype(jnp.int32))
-        s = jnp.where(seen, visits[zz] * SCALE2, FAR_BELOW)
+        s = jnp.where(seen, visits[zz], FAR_BELOW)
         p = jnp.exp2(s - rest[0:1])
         slopes = (p * (nt(own_values, visit_cot) - rest[1:2])).astype(BF16)
         return nn(slopes, visit), nn(p.astype(BF16), visit_cot)
@@ -400,7 +400,7 @@
         slopes = (p * (nt(own_cot, values_of(zz)) - delta)).astype(BF16)
         return nn(slopes, keys_of(zz))
 
-    visits[z] = nt(own_keys, query)
+    visits[z] = nt(own_keys, query) * SCALE2
     with scope("key_side_own"):
         dk[...], dv[...] = key_side(z)
     with scope("query_side_own"):
@@ -420,7 +420,7 @@
     def ahead(zz, _):
         arrived_q(zz, 0)
         arrived_q(zz, 1)
-        visits[zz] = nt(own_keys, qb[zz].reshape(256, HEAD_DIM))
+        visits[zz] = nt(own_keys, qb[zz].reshape(256, HEAD_DIM)) * SCALE2
         return 0
 
     lax.fori_loop(z + 1, 4, ahead, 0)
@@ -462,26 +462,42 @@
 
     lax.fori_loop(z + 1, 4, key_step, 0)
 
-    dk4 = dk.reshape(2, 2, 128, HEAD_DIM)
-    dv4 = dv.reshape(2, 2, 128, HEAD_DIM)
-    with scope("halves"):
-        half_out[0] = dk4[:, 1 - c].astype(BF16)
-        half_out[1] = dv4[:, 1 - c].astype(BF16)
-        half = send(half_out, half_in, half_send, half_recv, mate)
-        half.start()
-        half.wait_recv()
-    with scope("give_kv"):
-        give(2, ((dk4[:, c] + half_in[0]) * SCALE).astype(BF16))
-        give(3, (dv4[:, c] + half_in[1]).astype(BF16))
+    owners = [(1 - y, c), (1 - y, 1 - c), (y, 1 - c)]
+
+    def share_copy(number):
+        yy, cc = owners[number]
+        return send(
+            shares.at[yy, cc], got.at[y, c], share_send.at[number], share_recv.at[y, c],
+            at(z, yy, cc),
+        )
+
+    with scope("shares"):
+        for number, (yy, cc) in enumerate(owners + [(y, c)]):
+            keys = pl.ds(pl.multiple_of((2 * yy + cc) * 128, 128), 128)
+            shares[yy, cc, 0] = (dk[keys, :] * SCALE).astype(BF16)
+            shares[yy, cc, 1] = dv[keys, :].astype(BF16)
+            if number < 3:
+                share_copy(number).start()
+        got[y, c] = shares[y, c]
+    with scope("shares_wait"):
+        for yy, cc in owners:
+            send(
+                shares.at[0, 0], got.at[yy, cc], share_send.at[0], share_recv.at[yy, cc], mate
+            ).wait_recv()
+        for kind in range(2):
+            for h in range(2):
+                both = got[h, 0, kind].astype(F32) + got[h, 1, kind].astype(F32)
+                out_ref[2 + kind, h] = both.astype(BF16)
 
     with scope("out_wait"):
-        for number in range(4):
+        for number in range(2):
             out_keep(number).wait()
             out_copy(number).wait_recv()
 
-    for number in range(4):
+    for number in range(2):
         out_copy(number).wait_send()
-    half.wait_send()
+    for number in range(3):
+        share_copy(number).wait_send()
 
 
 def spread_kernel(blocks, *refs):
@@ -531,8 +547,8 @@
             vmem((256, 128), F32),
             vmem((512, 128), F32),
             vmem((512, 128), F32),
-            vmem((2, 2, 128, 128), BF16),
-            vmem((2, 2, 128, 128), BF16),
+            vmem((2, 2, 2, 128, 128), BF16),
+            vmem((2, 2, 2, 128, 128), BF16),
             vmem((4, 2, 128, 128), BF16),
             pltpu.SMEM((1,), jnp.int32), pltpu.SMEM((1,), jnp.int32),
             dma((10,)),
@@ -542,7 +558,7 @@
             dma((2, 4, 2)), dma((2, 4, 2)),
             dma((4,)), dma((4,)),
             dma, dma,
-            dma, dma,
+            dma((3,)), dma((2, 2)),
             dma((4,)), dma((4,)),
         ],
         compiler_params=pltpu.CompilerParams(

time: 34.7 us -> 34.7 us (level)
  no operation moved by 1% of the time
where the time goes in v4:
time: 34.7 us; the launch traced here: 34.6 us
  Pallas kernels  32.6 us (94%)
  between operations  1.93 us (6%)
    pallas_call x1, Pallas kernels, on_device(): pl.pallas_call(kernel, name='masked_attention', out_shape=pltpu.VMEM((4,...  31.9 us
    pallas_call x1, Pallas kernels, on_device(): pl.pallas_call(spread_kernel, name='spread_heads', out_shape=[jax.ShapeDt...  0.76 us

profile of v4, /device:TPU:1, one launch (start us, length us, event | category | flops | bytes accessed | tf_op | source)
XLA Modules:
  0.0 34.6 jit_solution(6010371670280583183)
XLA Ops:
  1.9 31.9 %masked_attention.1.blocks = bf16[4,2,128,128]{3,2,1,0:T(8,128)(2,1)S(1)} custom-call(bf16[128,256]{1,0:T(8,128)(2,1)} %q_hbm.1, bf16[128,256]{1,0:T(8,128)(2,1)} %k_hbm.1, bf16[128,256]{1,0:T(8,128)(2,1)} %v_hbm.1, s32[1]{0:T(128)S(6)} %copy.11.doc_hbm, s32[1]{0:T(128)S(6)} %copy.12.frame_hbm, bf16[16,4096]{1,0:T(8,128)(2,1)} %x_hbm.1, bf16[256,4096]{1,0:T(8,128)(2,1)} %w_hbm.1), custom_call_target="tpu_custom_call" | custom-call | tf_op jit(solution)/shard_map/masked_attention/pallas_call | solution.py:523
  33.8 0.8 %spread_heads.1 = (bf16[128,256]{1,0:T(8,128)(2,1)}, bf16[128,256]{1,0:T(8,128)(2,1)}, bf16[128,256]{1,0:T(8,128)(2,1)}, bf16[128,256]{1,0:T(8,128)(2,1)}) custom-call(bf16[4,2,128,128]{3,2,1,0:T(8,128)(2,1)S(1)} %masked_attention.1.blocks), custom_call_target="tpu_custom_call" | custom-call | tf_op jit(solution)/shard_map/spread_heads/pallas_call | solution.py:568

commit v5 on v3

--- a/solution.py
+++ b/solution.py
@@ -66,9 +66,6 @@
     )
 
     barrier = pltpu.get_barrier_semaphore()
-    for device in (x_up, x_down, x_far, y_far, mate):
-        pl.semaphore_signal(barrier, inc=1, device_id=device, device_id_type=MESH)
-
     def greet(i, _):
         zz, yy = i // 2, i % 2
 
@@ -79,6 +76,8 @@
         return 0
 
     lax.fori_loop(0, 8, greet, 0)
+    for device in (x_up, x_down, x_far, y_far, mate):
+        pl.semaphore_signal(barrier, inc=1, device_id=device, device_id_type=MESH)
 
     def head(ref, h):
         return ref.at[:, pl.ds(h * HEAD_DIM, HEAD_DIM)]

time: 34.7 us -> 34.6 us (level)
  no operation moved by 1% of the time
where the time goes in v5:
time: 34.6 us; the launch traced here: 34.5 us
  Pallas kernels  32.5 us (94%)
  between operations  1.93 us (6%)
    pallas_call x1, Pallas kernels, on_device(): pl.pallas_call(kernel, name='masked_attention', out_shape=pltpu.VMEM((4,...  31.8 us
    pallas_call x1, Pallas kernels, on_device(): pl.pallas_call(spread_kernel, name='spread_heads', out_shape=[jax.ShapeDt...  0.76 us

profile of v5, /device:TPU:1, one launch (start us, length us, event | category | flops | bytes accessed | tf_op | source)
XLA Modules:
  0.0 34.5 jit_solution(3373969887053595709)
XLA Ops:
  1.9 31.8 %masked_attention.1.blocks = bf16[4,2,128,128]{3,2,1,0:T(8,128)(2,1)S(1)} custom-call(bf16[128,256]{1,0:T(8,128)(2,1)} %q_hbm.1, bf16[128,256]{1,0:T(8,128)(2,1)} %k_hbm.1, bf16[128,256]{1,0:T(8,128)(2,1)} %v_hbm.1, s32[1]{0:T(128)S(6)} %copy.11.doc_hbm, s32[1]{0:T(128)S(6)} %copy.12.frame_hbm, bf16[16,4096]{1,0:T(8,128)(2,1)} %x_hbm.1, bf16[256,4096]{1,0:T(8,128)(2,1)} %w_hbm.1), custom_call_target="tpu_custom_call" | custom-call | tf_op jit(solution)/shard_map/masked_attention/pallas_call | solution.py:506
  33.7 0.8 %spread_heads.1 = (bf16[128,256]{1,0:T(8,128)(2,1)}, bf16[128,256]{1,0:T(8,128)(2,1)}, bf16[128,256]{1,0:T(8,128)(2,1)}, bf16[128,256]{1,0:T(8,128)(2,1)}) custom-call(bf16[4,2,128,128]{3,2,1,0:T(8,128)(2,1)S(1)} %masked_attention.1.blocks), custom_call_target="tpu_custom_call" | custom-call | tf_op jit(solution)/shard_map/spread_heads/pallas_call | solution.py:551
